TPU v7x, 32 devices: a whole 2x2x4 slice. The times are simulated.
32 devices in a mesh: seq: 8 (over z, x), head: 4 (over y, core).
Axes of the slice: x: 2, y: 2, z: 4, core: 2. Of those that a mesh axis runs over, the one named last changes fastest.
Arguments:
- inputs: bfloat16 [8192, 2048], P('seq', 'head'), may hold values from -6 to 6
- w_qkv: bfloat16 [3, 2048, 2048], P(None, None, 'head'), may hold values from -0.125 to 0.125
- level_weight: float32 [16, 4], P('head'), may hold values from 0.5 to 2
- grad_out: bfloat16 [8192, 2048], P('seq', 'head'), may hold values from -6 to 6
Outputs:
- attn_out: bfloat16 [8192, 2048], P('seq', 'head')
- grad_query: bfloat16 [8192, 2048], P('seq', 'head')
- grad_key: bfloat16 [8192, 2048], P('seq', 'head')
- grad_value: bfloat16 [8192, 2048], P('seq', 'head')
All inputs are finite; a program needn't handle non-finite values.
Results may differ from a plain program's by a relative error of at most 0.012.
Values may be sent and summed in bfloat16 or wider, within the bound.
No kernel may reach another device: no remote copies, remote signals or barrier semaphores. Data moves between devices by JAX's collectives and lax.ppermute only.
A program may use at most 128 MiB of HBM per device.

v0:
```python
import functools
import math

import jax
import jax.numpy as jnp
from jax import lax
from jax.experimental import pallas as pl
from jax.experimental.pallas import tpu as pltpu
from jax.sharding import PartitionSpec as P

SHARES = (10, 12, 13, 14, 15)
CHUNKS = len(SHARES)
GROUP = 4
MIB = 2**20
VMEM = pl.BlockSpec(memory_space=pltpu.VMEM)
SMEM = pl.BlockSpec(memory_space=pltpu.SMEM)
ANY = pl.BlockSpec(memory_space=pl.ANY)
HBM = pl.BlockSpec(memory_space=pltpu.HBM)
NN = (((1,), (0,)), ((), ()))
NT = (((1,), (1,)), ((), ()))
TN = (((0,), (0,)), ((), ()))
BF16 = jnp.bfloat16
F32 = jnp.float32


def dot(a, b, dims=NN):
    return lax.dot_general(a, b, dims, preferred_element_type=F32)


def swap(value, axis, mask):
    pairs = [(source, source ^ mask) for source in range(lax.axis_size(axis))]
    return lax.ppermute(value, axis, pairs)


def bit_of(position, bit):
    return lax.rem(position // 2**bit, 2) == 1


def call(kernel, outs, operands, specs, flops, scratch=(), out_specs=None, limit=4, moved=0):
    return pl.pallas_call(
        kernel,
        out_shape=outs,
        in_specs=specs,
        out_specs=[VMEM] * len(outs) if out_specs is None else out_specs,
        scratch_shapes=scratch,
        compiler_params=pltpu.CompilerParams(vmem_limit_bytes=limit * MIB),
        cost_estimate=pl.CostEstimate(flops=flops, bytes_accessed=moved, transcendentals=0),
    )(*operands)


def load_kernel(copied, *refs):
    count = 1 + max(source for source, _ in copied)
    sources, refs = refs[:count], refs[-len(copied) - 1 :]
    outs, sems = refs[:-1], refs[-1]
    copies = []
    for i, (source, start) in enumerate(copied):
        ref = sources[source]
        if start is not None:
            ref = ref.at[pl.ds(start, outs[i].shape[0])]
        copies.append(pltpu.make_async_copy(ref, outs[i], sems.at[i]))
    for copy in copies:
        copy.start()
    for copy in copies:
        copy.wait()


def load(sources, copied, after=()):
    shapes = []
    for source, span in copied:
        shape = sources[source].shape
        rows = shape[0] if span is None else span[1] - span[0]
        shapes.append(pltpu.VMEM((rows, *shape[1:]), BF16))
    copied = [(source, span if span is None else span[0]) for source, span in copied]
    return call(
        functools.partial(load_kernel, copied),
        shapes,
        [*[pltpu.with_memory_space_constraint(x, pltpu.HBM) for x in sources], *after],
        [HBM] * len(sources) + [ANY] * len(after),
        0,
        [pltpu.SemaphoreType.DMA((len(copied),))],
        limit=2,
        moved=4 * sum(math.prod(shape.shape) for shape in shapes),
    )


def tie_kernel(value_ref, *refs):
    del value_ref, refs


def tie(value, *after):
    return pl.pallas_call(
        tie_kernel,
        out_shape=pltpu.VMEM(value.shape, value.dtype),
        in_specs=[VMEM] + [ANY] * len(after),
        out_specs=VMEM,
        input_output_aliases={0: 0},
        compiler_params=pltpu.CompilerParams(vmem_limit_bytes=MIB),
    )(value, *after)


def project(w_ref, segments, j):
    me = lax.axis_index("head")
    parts = lax.axis_size("head")
    depth = w_ref.shape[1] // parts
    total = None
    for k, rows in segments:
        start = pl.multiple_of((me ^ k) * depth, depth)
        term = dot(rows, w_ref[j, pl.ds(start, depth), :])
        total = term if total is None else total + term
    return total


def read_segments(refs, keys, span):
    found = []
    for k, ref in zip(keys, refs):
        whole = ref.shape[0] != span[1] - span[0]
        found.append((k, ref[span[0] : span[1], :] if whole else ref[...]))
    return found


def early_kernel(keys, span, w_ref, *refs):
    segments, total_ref = refs[:-1], refs[-1]
    for j in range(3):
        total_ref[j] = project(w_ref, read_segments(segments, keys, span), j)


def project_kernel(keys, span, heads, w_ref, g_ref, *refs):
    segments, refs = refs[: len(keys)], refs[len(keys) :]
    q_ref, k_ref, v_ref, state_ref = refs[-4:]
    for j, out_ref in enumerate((q_ref, k_ref, v_ref)):
        out_ref[...] = project(w_ref, read_segments(segments, keys, span), j).astype(BF16)
    size = q_ref.shape[1] // heads
    for h in range(heads):
        cols = slice(h * size, (h + 1) * size)
        state_ref[0, h] = dot(k_ref[:, cols], v_ref[:, cols], TN)
        state_ref[1, h] = dot(q_ref[:, cols], g_ref[span[0] : span[1], cols], TN)


def last_kernel(keys, span, heads, w_ref, g_ref, part_ref, *refs):
    segments, refs = refs[: len(keys)], refs[len(keys) :]
    earlier, refs = refs[: -6 - (GROUP - 1)], refs[-6 - (GROUP - 1) :]
    q_ref, k_ref, v_ref, state_ref, total_ref, near_ref, *sends = refs
    for j, out_ref in enumerate((q_ref, k_ref, v_ref)):
        term = project(w_ref, read_segments(segments, keys, span), j)
        out_ref[...] = (part_ref[j] + term).astype(BF16)
    size = q_ref.shape[1] // heads
    share = heads // GROUP
    place = lax.rem(lax.axis_index("seq"), GROUP)
    for h in range(heads):
        cols = slice(h * size, (h + 1) * size)
        state_ref[0, h] = dot(k_ref[:, cols], v_ref[:, cols], TN)
        state_ref[1, h] = dot(q_ref[:, cols], g_ref[span[0] : span[1], cols], TN)
        for s in range(2):
            total = state_ref[s, h]
            for other in earlier:
                total = total + other[s, h]
            total_ref[s, h] = total
    for m, send in enumerate(sends, 1):
        for s in range(2):
            for e in range(share):
                send[s, e] = total_ref[s, (place ^ m) * share + e].astype(BF16)
    odd = bit_of(lax.axis_index("seq"), 0)
    for h in range(heads):
        near_ref[h] = jnp.where(odd, total_ref[1, h], total_ref[0, h]).astype(BF16)


def local_kernel(span, heads, weight_ref, q_ref, k_ref, v_ref, g_ref, after_ref, out_ref):
    rows = q_ref.shape[0]
    size = q_ref.shape[1] // heads
    norm = 1.0 / math.sqrt(size * g_ref.shape[0])
    at = lax.broadcasted_iota(jnp.int32, (rows, rows), 0)
    of = lax.broadcasted_iota(jnp.int32, (rows, rows), 1)
    columns = [slice(h * size, (h + 1) * size) for h in range(heads)]
    masked = []
    for h, cols in enumerate(columns):
        q, k, v = q_ref[:, cols], k_ref[:, cols], v_ref[:, cols]
        g = g_ref[span[0] : span[1], cols]
        scale = weight_ref[h, 0] * norm
        found = []
        for left, right, causal in (
            (q, k, at >= of),
            (g, v, at >= of),
            (v, g, of >= at),
            (k, q, of >= at),
        ):
            found.append(jnp.where(causal, dot(left, right, NT) * scale, 0.0).astype(BF16))
        masked.append(found)
    for h, cols in enumerate(columns):
        q, k, v = q_ref[:, cols], k_ref[:, cols], v_ref[:, cols]
        g = g_ref[span[0] : span[1], cols]
        for j, value in enumerate((v, k, q, g)):
            out_ref[j, :, cols] = dot(masked[h][j], value)


def owner_kernel(final, total_ref, *refs):
    got, (near_ref, far_ref, sum_ref, next_ref) = refs[: GROUP - 1], refs[-4:]
    position = lax.axis_index("seq")
    place = lax.rem(position, GROUP)
    share = total_ref.shape[1] // GROUP
    high = bit_of(position, 1)
    for e in range(share):
        mine, other = [], []
        for s in range(2):
            mine.append(total_ref[s, place * share + e] + got[0][s, e].astype(F32))
            other.append(got[1][s, e].astype(F32) + got[2][s, e].astype(F32))
        near_ref[e] = jnp.where(high, other[0], other[1]).astype(BF16)
        far_ref[e] = jnp.where(high, mine[1], mine[0]).astype(BF16)
        sums = [mine[s] + other[s] for s in range(2)]
        write_next(sums, e, 2, final, sum_ref, next_ref)


def write_next(sums, e, bit, final, sum_ref, next_ref):
    if final:
        value = jnp.where(bit_of(lax.axis_index("seq"), bit), sums[1], sums[0])
        next_ref[e] = value.astype(BF16)
        return
    for s in range(2):
        sum_ref[s, e] = sums[s]
        next_ref[s, e] = sums[s].astype(BF16)


def climb_kernel(bit, next_final, got_ref, old_ref, level_ref, sum_ref, next_ref):
    on = bit_of(lax.axis_index("seq"), bit)
    for e in range(got_ref.shape[1]):
        both = [got_ref[s, e].astype(F32) for s in range(2)]
        level_ref[e] = jnp.where(on, both[0], both[1]).astype(BF16)
        sums = [old_ref[s, e] + both[s] for s in range(2)]
        write_next(sums, e, bit + 1, next_final, sum_ref, next_ref)


def pair_block(first, second):
    zero = jnp.zeros(first.shape, BF16)
    top = jnp.concatenate([first.astype(BF16), zero], axis=1)
    bottom = jnp.concatenate([zero, second.astype(BF16)], axis=1)
    return jnp.concatenate([top, bottom], axis=0)


def finish_kernel(spans, heads, groups, weight_ref, g_ref, near_ref, *refs):
    chunks = len(spans)
    levels, refs = refs[: groups * GROUP], refs[groups * GROUP :]
    q_refs, refs = refs[:chunks], refs[chunks:]
    k_refs, refs = refs[:chunks], refs[chunks:]
    v_refs, refs = refs[:chunks], refs[chunks:]
    state_refs, refs = refs[:chunks], refs[chunks:]
    part_refs, refs = refs[:chunks], refs[chunks:]
    outs, (held, mix_ref, sems) = refs[:4], refs[4:]
    position = lax.axis_index("seq")
    place = lax.rem(position, GROUP)
    size = q_refs[0].shape[1] // heads
    share = heads // GROUP
    block = g_ref.shape[0]
    norm = 1.0 / math.sqrt(size * block)
    for m in range(GROUP):
        for e in range(share):
            h = (place ^ m) * share + e
            values = [near_ref[h]] + [levels[b * GROUP + m][e] for b in range(groups)]
            forward = backward = None
            for level, value in enumerate(values):
                coef = weight_ref[h, level + 1] * (1.0 / math.sqrt(size * block * 2**level))
                on = bit_of(position, level)
                value = value.astype(F32)
                to_forward = jnp.where(on, coef, 0.0) * value
                to_backward = jnp.where(on, 0.0, coef) * value
                forward = to_forward if forward is None else forward + to_forward
                backward = to_backward if backward is None else backward + to_backward
            mix_ref[0, h] = forward
            mix_ref[1, h] = backward
    copies = []
    for s in range(2):
        sums = [mix_ref[s, h] for h in range(heads)]
        for c in range(chunks) if s == 0 else reversed(range(chunks)):
            span = slice(*spans[c])
            weights = [pair_block(sums[h], sums[h + 1]) for h in range(0, heads, 2)]
            for j in (2 * s, 2 * s + 1):
                for h in range(0, heads, 2):
                    cols = slice(h * size, (h + 2) * size)
                    weight = weights[h // 2]
                    if j == 0:
                        term = dot(q_refs[c][:, cols], weight)
                    elif j == 1:
                        term = dot(g_ref[span, cols], weight, NT)
                    elif j == 2:
                        term = dot(v_refs[c][:, cols], weight, NT)
                    else:
                        term = dot(k_refs[c][:, cols], weight)
                    held[j, span, cols] = (term + part_refs[c][j, :, cols]).astype(BF16)
                copy = pltpu.make_async_copy(held.at[j, span], outs[j].at[span], sems.at[j, c])
                copy.start()
                copies.append(copy)
            sums = [
                total + weight_ref[h, 0] * norm * state_refs[c][s, h]
                for h, total in enumerate(sums)
            ]
    for copy in copies:
        copy.wait()


def exchange(totals, near, sends, local, late):
    depth = lax.axis_size("seq").bit_length() - 1
    heads, square = totals.shape[1], totals.shape[2:]
    share = heads // GROUP
    last = depth - 1

    def message(bit):
        return pltpu.VMEM((share, *square) if bit == last else (2, share, *square), BF16)

    def running(bit):
        return pltpu.VMEM((1, 8, 128) if bit == last else (2, share, *square), F32)

    def spread(mine, other):
        return [mine, *[swap(mine if m == 1 else other, "seq", m) for m in range(1, GROUP)]]

    one = pltpu.VMEM((share, *square), BF16)
    got = [swap(send, "seq", m) for m, send in enumerate(sends, 1)]
    near = swap(near, "seq", 1)
    fillers = [local(late[0], sends[0])]
    mine, other, sums, sent = call(
        functools.partial(owner_kernel, last == 2),
        [one, one, running(2), message(2)],
        [totals, *got, fillers[0]],
        [VMEM] * GROUP + [ANY],
        10**6,
    )
    levels = spread(mine, other)
    for bit in range(2, last):
        found, sums, sent = call(
            functools.partial(climb_kernel, bit, bit + 1 == last),
            [one, running(bit + 1), message(bit + 1)],
            [swap(sent, "seq", 1 << bit), sums],
            [VMEM] * 2,
            10**6,
        )
        levels += spread(found, found)
    found = tie(swap(sent, "seq", 1 << last), near, *levels)
    levels += spread(found, found)
    fillers += [local(c, found) for c in late[1:]]
    return near, levels, fillers


def per_device(inputs, w_qkv, level_weight, grad_out):
    rows, width = grad_out.shape
    heads = level_weight.shape[0]
    size = width // heads
    parts = lax.axis_size("head")
    edges = [rows * sum(SHARES[:c]) // sum(SHARES) for c in range(CHUNKS + 1)]
    spans = list(zip(edges[:-1], edges[1:]))
    copied = [(0, span) for span in spans]
    mine = load([inputs], copied[:1])
    mine = [*mine, *load([inputs], copied[1:], mine)]
    grads, weights = load([grad_out, w_qkv], [(0, None), (1, None)], mine[1:2])
    top, *lows = [1 << b for b in reversed(range(parts.bit_length() - 1))]
    arrived = [swap(piece, "head", top) for piece in mine]
    arrived[0] = tie(arrived[0], weights)
    whole = {0: inputs}
    for low in lows:
        for k in sorted(whole):
            whole[k | low] = swap(whole[k], "head", low)
    state = pltpu.VMEM((2, heads, size, size), F32)
    qs, ks, vs, states, locals_ = [], [], [], [], []

    def local(c, after):
        chunk = spans[c][1] - spans[c][0]
        return call(
            functools.partial(local_kernel, spans[c], heads),
            [pltpu.VMEM((4, chunk, width), F32)],
            [level_weight, qs[c], ks[c], vs[c], grads, after],
            [SMEM] + [VMEM] * 4 + [ANY],
            100 * chunk * chunk * width if c >= CHUNKS - 2 else 0,
        )[0]

    after = None
    for c in range(CHUNKS):
        pieces = {**whole, 0: mine[c]}
        pieces[top] = arrived[c] if after is None else tie(arrived[c], after)
        for low in lows:
            for k in [k for k in sorted(pieces) if k & top]:
                pieces[k | low] = swap(pieces[k], "head", low)
        keys = sorted(pieces)
        chunk = spans[c][1] - spans[c][0]
        flat = pltpu.VMEM((chunk, width), BF16)
        flops = 0
        if c < CHUNKS - 1:
            if c > 0:
                locals_.append(local(c - 1, pieces[top]))
            operands = [weights, grads, *[pieces[k] for k in keys], *locals_[-1:]]
            got = call(
                functools.partial(project_kernel, keys, spans[c], heads),
                [flat, flat, flat, state],
                operands,
                [VMEM] * (2 + len(keys)) + [ANY] * len(locals_[-1:]),
                flops * len(keys),
            )
        else:
            early, late = keys[:-1], keys[-1:]
            (begun,) = call(
                functools.partial(early_kernel, early, spans[c]),
                [pltpu.VMEM((3, chunk, width), F32)],
                [weights, *[pieces[k] for k in early]],
                [VMEM] * (1 + len(early)),
                flops * len(early),
            )
            operands = [weights, grads, begun, *[pieces[k] for k in late], *states]
            got = call(
                functools.partial(last_kernel, late, spans[c], heads),
                [
                    flat,
                    flat,
                    flat,
                    state,
                    state,
                    pltpu.VMEM((heads, size, size), BF16),
                    *[pltpu.VMEM((2, heads // GROUP, size, size), BF16)] * (GROUP - 1),
                ],
                operands,
                [VMEM] * len(operands),
                flops * len(late),
            )
        qs.append(got[0])
        ks.append(got[1])
        vs.append(got[2])
        states.append(got[3])
        after = got[3]
    near, levels, fillers = exchange(got[4], got[5], got[6:], local, range(len(locals_), CHUNKS))
    locals_ += fillers
    operands = [level_weight, grads, near, *levels, *qs, *ks, *vs, *states, *locals_]
    return call(
        functools.partial(finish_kernel, spans, heads, len(levels) // GROUP),
        [jax.ShapeDtypeStruct((rows, width), BF16)] * 4,
        operands,
        [SMEM] + [VMEM] * (len(operands) - 1),
        16 * rows * size * width,
        [
            pltpu.VMEM((4, rows, width), BF16),
            pltpu.VMEM((2, heads, size, size), F32),
            pltpu.SemaphoreType.DMA((4, CHUNKS)),
        ],
        [ANY] * 4,
        12,
    )


def solution(mesh):
    in_specs = (P("seq", "head"), P(None, None, "head"), P("head", None), P("seq", "head"))
    out_specs = (P("seq", "head"), P("seq", "head"), P("seq", "head"), P("seq", "head"))
    return jax.shard_map(
        per_device, mesh=mesh, in_specs=in_specs, out_specs=out_specs, check_vma=False
    )
```

profile of v0, /device:TPU:0, one launch (start us, length us, event | category | flops | bytes accessed | tf_op | source)
XLA Modules:
  0.0 58.8 jit_solution(10454939047284785596)
XLA Ops:
  0.6 0.5 collective-permute-start
  1.1 0.9 %shard_map.75.refs_1_.refs_0_ = bf16[160,512]{1,0:T(8,128)(2,1)S(1)} custom-call(bf16[1024,512]{1,0:T(8,128)(2,1)} %refs_0_.4), custom_call_target="tpu_custom_call" | custom-call | bytes 327680 | tf_op jit(solution)/shard_map/pallas_call | solution.py:40
  2.1 2.6 %collective-permute-start.5 = (bf16[160,512]{1,0:T(8,128)(2,1)S(1)}, bf16[160,512]{1,0:T(8,128)(2,1)S(1)}, u32[]{:S(2)}, u32[]{:S(2)}) collective-permute-start(bf16[160,512]{1,0:T(8,128)(2,1)S(1)} %shard_map.75.refs_1_.refs_0_), channel_id=1, source_target_pairs={{0,2},{1,3},{2,0},{3,1},{4,6},{5,7},{6,4},{7,5},{8,10},{9,11},{10,... | collective-permute-start | bytes 491528 | tf_op jit(solution)/shard_map/ppermute | solution.py:32
  4.7 1.3 %shard_map.76 = (bf16[192,512]{1,0:T(8,128)(2,1)S(1)}, bf16[208,512]{1,0:T(8,128)(2,1)S(1)}, bf16[224,512]{1,0:T(8,128)(2,1)S(1)}, bf16[240,512]{1,0:T(8,128)(2,1)S(1)}) custom-call(bf16[1024,512]{1,0:T(8,128)(2,1)} %refs_0_.4, bf16[160,512]{1,0:T(8,128)(2,1)S(1)} %shard_map.75.refs_1_.refs_0_), custom_call_target="tpu_custom_call" | custom-call | bytes 1769472 | tf_op jit(solution)/shard_map/pallas_call | solution.py:40
  6.0 0.1 collective-permute-start.4
  6.1 3.1 %shard_map.77 = (bf16[1024,512]{1,0:T(8,128)(2,1)S(1)}, bf16[3,2048,512]{2,1,0:T(8,128)(2,1)S(1)}) custom-call(bf16[1024,512]{1,0:T(8,128)(2,1)} %refs_0_.5, bf16[3,2048,512]{2,1,0:T(8,128)(2,1)} %refs_1_.1, bf16[192,512]{1,0:T(8,128)(2,1)S(1)} %get-tuple-element.38.refs_2_.refs_0_), custom_call_target="tpu_custom_call" | custom-call | bytes 14680064 | tf_op jit(solution)/shard_map/pallas_call | solution.py:40
  9.2 0.5 collective-permute-done.5.value_ref
  9.7 0.0 collective-permute-start.6
  9.7 1.9 %collective-permute-start.3 = (bf16[208,512]{1,0:T(8,128)(2,1)S(1)}, bf16[208,512]{1,0:T(8,128)(2,1)S(1)}, u32[]{:S(2)}, u32[]{:S(2)}) collective-permute-start(bf16[208,512]{1,0:T(8,128)(2,1)S(1)} %get-tuple-element.43.refs_0_), channel_id=1, source_target_pairs={{0,2},{1,3},{2,0},{3,1},{4,6},{5,7},{6,4},{7,5},{8,10},{9,11},{10,... | collective-permute-start | bytes 638984 | tf_op jit(solution)/shard_map/ppermute | solution.py:32
  11.7 1.5 %shard_map.79 = (bf16[160,512]{1,0:T(8,128)(2,1)S(1)}, bf16[160,512]{1,0:T(8,128)(2,1)S(1)}, bf16[160,512]{1,0:T(8,128)(2,1)S(1)}, f32[2,4,128,128]{3,2,1,0:T(8,128)S(1)}) custom-call(bf16[3,2048,512]{2,1,0:T(8,128)(2,1)S(1)} %get-tuple-element.40.refs_0_.w_ref, bf16[1024,512]{1,0:T(8,128)(2,1)S(1)} %get-tuple-element.39.g_ref, ...), custom_call_target="tpu_custom_call" | custom-call | tf_op jit(solution)/shard_map/pallas_call | solution.py:40
  13.2 0.7 %collective-permute-done.4.value_ref = bf16[192,512]{1,0:T(8,128)(2,1)S(1)} collective-permute-done((bf16[192,512]{1,0:T(8,128)(2,1)S(1)}, bf16[192,512]{1,0:T(8,128)(2,1)S(1)}, u32[]{:S(2)}, u32[]{:S(2)}) %collective-permute-start.4) | collective-permute-done | bytes 196640 | tf_op jit(solution)/shard_map/ppermute | solution.py:32
  13.9 0.0 collective-permute-start.7
  13.9 1.9 %collective-permute-start.2 = (bf16[224,512]{1,0:T(8,128)(2,1)S(1)}, bf16[224,512]{1,0:T(8,128)(2,1)S(1)}, u32[]{:S(2)}, u32[]{:S(2)}) collective-permute-start(bf16[224,512]{1,0:T(8,128)(2,1)S(1)} %get-tuple-element.42.refs_0_), channel_id=1, source_target_pairs={{0,2},{1,3},{2,0},{3,1},{4,6},{5,7},{6,4},{7,5},{8,10},{9,11},{10,... | collective-permute-start | bytes 688136 | tf_op jit(solution)/shard_map/ppermute | solution.py:32
  15.9 1.4 %shard_map.81.refs_4_.refs_28_ = f32[4,160,512]{2,1,0:T(8,128)S(1)} custom-call(f32[4,4]{1,0:T(4,128)S(1)} %copy-done, bf16[160,512]{1,0:T(8,128)(2,1)S(1)} %get-tuple-element.45.q_ref.refs_8_, bf16[160,512]{1,0:T(8,128)(2,1)S(1)} %get-tuple-element.46.k_ref.refs_13_, bf16[160,512]{1,0:T(8,128)(2,1)S(1)} %get-tuple-element.47.v_ref.refs_18_, ...), custom_call_target="tpu_custom_call" | custom-call | tf_op jit(solution)/shard_map/pallas_call | solution.py:40
  17.3 1.7 %shard_map.82 = (bf16[192,512]{1,0:T(8,128)(2,1)S(1)}, bf16[192,512]{1,0:T(8,128)(2,1)S(1)}, bf16[192,512]{1,0:T(8,128)(2,1)S(1)}, f32[2,4,128,128]{3,2,1,0:T(8,128)S(1)}) custom-call(bf16[3,2048,512]{2,1,0:T(8,128)(2,1)S(1)} %get-tuple-element.40.refs_0_.w_ref, bf16[1024,512]{1,0:T(8,128)(2,1)S(1)} %get-tuple-element.39.g_ref, ...), custom_call_target="tpu_custom_call" | custom-call | tf_op jit(solution)/shard_map/pallas_call | solution.py:40
  19.1 0.3 collective-permute-start.8
  19.4 1.1 %collective-permute-start.1 = (bf16[240,512]{1,0:T(8,128)(2,1)S(1)}, bf16[240,512]{1,0:T(8,128)(2,1)S(1)}, u32[]{:S(2)}, u32[]{:S(2)}) collective-permute-start(bf16[240,512]{1,0:T(8,128)(2,1)S(1)} %get-tuple-element.41.refs_0_), channel_id=1, source_target_pairs={{0,2},{1,3},{2,0},{3,1},{4,6},{5,7},{6,4},{7,5},{8,10},{9,11},{10,... | collective-permute-start | bytes 737288 | tf_op jit(solution)/shard_map/ppermute | solution.py:32
  20.5 1.6 %shard_map.84.refs_4_.refs_29_ = f32[4,192,512]{2,1,0:T(8,128)S(1)} custom-call(f32[4,4]{1,0:T(4,128)S(1)} %copy-done, bf16[192,512]{1,0:T(8,128)(2,1)S(1)} %get-tuple-element.49.q_ref.refs_9_, bf16[192,512]{1,0:T(8,128)(2,1)S(1)} %get-tuple-element.50.k_ref.refs_14_, bf16[192,512]{1,0:T(8,128)(2,1)S(1)} %get-tuple-element.51.v_ref.refs_19_, ...), custom_call_target="tpu_custom_call" | custom-call | tf_op jit(solution)/shard_map/pallas_call | solution.py:40
  22.1 1.8 %shard_map.85 = (bf16[208,512]{1,0:T(8,128)(2,1)S(1)}, bf16[208,512]{1,0:T(8,128)(2,1)S(1)}, bf16[208,512]{1,0:T(8,128)(2,1)S(1)}, f32[2,4,128,128]{3,2,1,0:T(8,128)S(1)}) custom-call(bf16[3,2048,512]{2,1,0:T(8,128)(2,1)S(1)} %get-tuple-element.40.refs_0_.w_ref, bf16[1024,512]{1,0:T(8,128)(2,1)S(1)} %get-tuple-element.39.g_ref, ...), custom_call_target="tpu_custom_call" | custom-call | tf_op jit(solution)/shard_map/pallas_call | solution.py:40
  23.9 0.3 collective-permute-start.9
  24.2 1.6 %shard_map.87.refs_4_.refs_30_ = f32[4,208,512]{2,1,0:T(8,128)S(1)} custom-call(f32[4,4]{1,0:T(4,128)S(1)} %copy-done, bf16[208,512]{1,0:T(8,128)(2,1)S(1)} %get-tuple-element.53.q_ref.refs_10_, bf16[208,512]{1,0:T(8,128)(2,1)S(1)} %get-tuple-element.54.k_ref.refs_15_, bf16[208,512]{1,0:T(8,128)(2,1)S(1)} %get-tuple-element.55.v_ref.refs_20_, ...), custom_call_target="tpu_custom_call" | custom-call | tf_op jit(solution)/shard_map/pallas_call | solution.py:40
  25.9 1.9 %shard_map.88 = (bf16[224,512]{1,0:T(8,128)(2,1)S(1)}, bf16[224,512]{1,0:T(8,128)(2,1)S(1)}, bf16[224,512]{1,0:T(8,128)(2,1)S(1)}, f32[2,4,128,128]{3,2,1,0:T(8,128)S(1)}) custom-call(bf16[3,2048,512]{2,1,0:T(8,128)(2,1)S(1)} %get-tuple-element.40.refs_0_.w_ref, bf16[1024,512]{1,0:T(8,128)(2,1)S(1)} %get-tuple-element.39.g_ref, ...), custom_call_target="tpu_custom_call" | custom-call | tf_op jit(solution)/shard_map/pallas_call | solution.py:40
  27.8 0.7 %collective-permute-done.1.value_ref = bf16[240,512]{1,0:T(8,128)(2,1)S(1)} collective-permute-done((bf16[240,512]{1,0:T(8,128)(2,1)S(1)}, bf16[240,512]{1,0:T(8,128)(2,1)S(1)}, u32[]{:S(2)}, u32[]{:S(2)}) %collective-permute-start.1) | collective-permute-done | bytes 245792 | tf_op jit(solution)/shard_map/ppermute | solution.py:32
  28.5 1.3 %shard_map.90.part_ref = f32[3,240,512]{2,1,0:T(8,128)S(1)} custom-call(bf16[3,2048,512]{2,1,0:T(8,128)(2,1)S(1)} %get-tuple-element.40.refs_0_.w_ref, bf16[240,512]{1,0:T(8,128)(2,1)S(1)} %get-tuple-element.41.refs_0_, bf16[1024,512]{1,0:T(8,128)(2,1)S(1)} %collective-permute-done.refs_1_, bf16[240,512]{1,0:T(8,128)(2,1)S(1)} %shard_map.89.refs_2_), custom_call_target="tpu_custom_call" | custom-call | tf_op jit(solution)/shard_map/pallas_call | solution.py:40
  29.8 0.2 collective-permute-done.10.refs_0_
  30.0 0.9 %shard_map.91 = (bf16[240,512]{1,0:T(8,128)(2,1)S(1)}, bf16[240,512]{1,0:T(8,128)(2,1)S(1)}, bf16[240,512]{1,0:T(8,128)(2,1)S(1)}, f32[2,4,128,128]{3,2,1,0:T(8,...) custom-call(bf16[3,2048,512]{2,1,0:T(8,128)(2,1)S(1)} %get-tuple-ele, ...), custom_call_target="tpu_custom_call" | custom-call | tf_op jit(solution)/shard_map/pallas_call | solution.py:40
  30.9 1.9 %collective-permute-start.13 = (bf16[2,1,128,128]{3,2,1,0:T(8,128)(2,1)S(1)}, bf16[2,1,128,128]{3,2,1,0:T(8,128)(2,1)S(1)}, u32[]{:S(2)}, u32[]{:S(2)}) collective-permute-start(bf16[2,1,128,128]{3,2,1,0:T(8,128)(2,1)S(1)} %get-tuple-element.60), channel_id=1, source_target_pairs={{0,8},{4,12},{8,0},{12,4},{16,24},{20,28},{24,16},{28,20},{1,9},{5... | collective-permute-start | bytes 196616 | tf_op jit(solution)/shard_map/ppermute | solution.py:32
  32.8 1.4 %collective-permute-start.14 = (bf16[2,1,128,128]{3,2,1,0:T(8,128)(2,1)S(1)}, bf16[2,1,128,128]{3,2,1,0:T(8,128)(2,1)S(1)}, u32[]{:S(2)}, u32[]{:S(2)}) collective-permute-start(bf16[2,1,128,128]{3,2,1,0:T(8,128)(2,1)S(1)} %get-tuple-element.61), channel_id=1, source_target_pairs={{0,12},{4,8},{8,4},{12,0},{16,28},{20,24},{24,20},{28,16},{1,13},{... | collective-permute-start | bytes 196616 | tf_op jit(solution)/shard_map/ppermute | solution.py:32
  34.2 0.3 collective-permute-start.12
  34.5 1.7 %collective-permute-start.11 = (bf16[4,128,128]{2,1,0:T(8,128)(2,1)S(1)}, bf16[4,128,128]{2,1,0:T(8,128)(2,1)S(1)}, u32[]{:S(2)}, u32[]{:S(2)}) collective-permute-start(bf16[4,128,128]{2,1,0:T(8,128)(2,1)S(1)} %get-tuple-element.57), channel_id=1, source_target_pairs={{0,4},{4,0},{8,12},{12,8},{16,20},{20,16},{24,28},{28,24},{1,5},{5... | collective-permute-start | bytes 393224 | tf_op jit(solution)/shard_map/ppermute | solution.py:32
  36.2 1.7 %shard_map.92.refs_3_.refs_31_ = f32[4,224,512]{2,1,0:T(8,128)S(1)} custom-call(f32[4,4]{1,0:T(4,128)S(1)} %copy-done, bf16[224,512]{1,0:T(8,128)(2,1)S(1)} %get-tuple-element.62.q_ref.refs_11_, bf16[224,512]{1,0:T(8,128)(2,1)S(1)} %get-tuple-element.63.k_ref.refs_16_, bf16[224,512]{1,0:T(8,128)(2,1)S(1)} %get-tuple-element.64.v_ref.refs_21_, ...), custom_call_target="tpu_custom_call" | custom-call | flops 2569011200 | tf_op jit(solution)/shard_map/pallas_call | solution.py:40
  37.9 0.1 collective-permute-done.14.refs_2_
  38.0 1.4 %collective-permute-done.12.refs_0_ = bf16[2,1,128,128]{3,2,1,0:T(8,128)(2,1)S(1)} collective-permute-done((bf16[2,1,128,128]{3,2,1,0:T(8,128)(2,1)S(1)}, bf16[2,1,128,128]{3,2,1,0:T(8,128)(2,1)S(1)}, u32[]{:S(2)}, u32[]{:S(2)}) %collective-permute-start.12) | collective-permute-done | bytes 65568 | tf_op jit(solution)/shard_map/ppermute | solution.py:32
  39.4 0.6 %shard_map.93 = (bf16[1,128,128]{2,1,0:T(8,128)(2,1)S(1)}, bf16[1,128,128]{2,1,0:T(8,128)(2,1)S(1)}, f32[1,8,128]{2,1,0:T(8,128)}, bf16[1,128,128]{2,1,0:T(8,128)(2,1)S(1)}) custom-call(f32[2,4,128,128]{3,2,1,0:T(8,128)S(1)} %get-tuple-element.58.total_ref, bf16[2,1,128,128]{3,2,1,0:T(8,128)(2,1)S(1)} %collective-permute-done.12.refs_0_, ...), custom_call_target="tpu_custom_call" | custom-call | flops 1000000 | tf_op jit(solution)/shard_map/pallas_call | solution.py:40
  40.0 2.6 %collective-permute-start.18 = (bf16[1,128,128]{2,1,0:T(8,128)(2,1)S(1)}, bf16[1,128,128]{2,1,0:T(8,128)(2,1)S(1)}, u32[]{:S(2)}, u32[]{:S(2)}) collective-permute-start(bf16[1,128,128]{2,1,0:T(8,128)(2,1)S(1)} %get-tuple-element.67), channel_id=1, source_target_pairs={{0,16},{4,20},{8,24},{12,28},{16,0},{20,4},{24,8},{28,12},{1,17},{... | collective-permute-start | bytes 98312 | tf_op jit(solution)/shard_map/ppermute | solution.py:32
  42.6 1.5 %collective-permute-start.17 = (bf16[1,128,128]{2,1,0:T(8,128)(2,1)S(1)}, bf16[1,128,128]{2,1,0:T(8,128)(2,1)S(1)}, u32[]{:S(2)}, u32[]{:S(2)}) collective-permute-start(bf16[1,128,128]{2,1,0:T(8,128)(2,1)S(1)} %get-tuple-element.66), channel_id=1, source_target_pairs={{0,12},{4,8},{8,4},{12,0},{16,28},{20,24},{24,20},{28,16},{1,13},{... | collective-permute-start | bytes 98312 | tf_op jit(solution)/shard_map/ppermute | solution.py:32
  44.1 1.2 %collective-permute-start.16 = (bf16[1,128,128]{2,1,0:T(8,128)(2,1)S(1)}, bf16[1,128,128]{2,1,0:T(8,128)(2,1)S(1)}, u32[]{:S(2)}, u32[]{:S(2)}) collective-permute-start(bf16[1,128,128]{2,1,0:T(8,128)(2,1)S(1)} %get-tuple-element.66), channel_id=1, source_target_pairs={{0,8},{4,12},{8,0},{12,4},{16,24},{20,28},{24,16},{28,20},{1,9},{5... | collective-permute-start | bytes 98312 | tf_op jit(solution)/shard_map/ppermute | solution.py:32
  45.3 0.8 %collective-permute-start.15 = (bf16[1,128,128]{2,1,0:T(8,128)(2,1)S(1)}, bf16[1,128,128]{2,1,0:T(8,128)(2,1)S(1)}, u32[]{:S(2)}, u32[]{:S(2)}) collective-permute-start(bf16[1,128,128]{2,1,0:T(8,128)(2,1)S(1)} %get-tuple-element.65.refs_1_.refs_0_), channel_id=1, source_target_pairs={{0,4},{4,0},{8,12},{12,8},{16,20},{20,16},{24,28},{28,24},{1,5},{5... | collective-permute-start | bytes 98312 | tf_op jit(solution)/shard_map/ppermute | solution.py:32
  46.1 1.3 %collective-permute-done.17.refs_4_.refs_3_ = bf16[1,128,128]{2,1,0:T(8,128)(2,1)S(1)} collective-permute-done((bf16[1,128,128]{2,1,0:T(8,128)(2,1)S(1)}, bf16[1,128,128]{2,1,0:T(8,128)(2,1)S(1)}, u32[]{:S(2)}, u32[]{:S(2)}) %collective-permute-start.17) | collective-permute-done | bytes 32800 | tf_op jit(solution)/shard_map/ppermute | solution.py:32
  47.4 0.6 %collective-permute-done.16.refs_3_.refs_2_ = bf16[1,128,128]{2,1,0:T(8,128)(2,1)S(1)} collective-permute-done((bf16[1,128,128]{2,1,0:T(8,128)(2,1)S(1)}, bf16[1,128,128]{2,1,0:T(8,128)(2,1)S(1)}, u32[]{:S(2)}, u32[]{:S(2)}) %collective-permute-start.16) | collective-permute-done | bytes 32800 | tf_op jit(solution)/shard_map/ppermute | solution.py:32
  48.0 1.2 %collective-permute-done.15.refs_2_.refs_1_ = bf16[1,128,128]{2,1,0:T(8,128)(2,1)S(1)} collective-permute-done((bf16[1,128,128]{2,1,0:T(8,128)(2,1)S(1)}, bf16[1,128,128]{2,1,0:T(8,128)(2,1)S(1)}, u32[]{:S(2)}, u32[]{:S(2)}) %collective-permute-start.15) | collective-permute-done | bytes 32800 | tf_op jit(solution)/shard_map/ppermute | solution.py:32
  49.2 1.8 %collective-permute-start.21 = (bf16[1,128,128]{2,1,0:T(8,128)(2,1)S(1)}, bf16[1,128,128]{2,1,0:T(8,128)(2,1)S(1)}, u32[]{:S(2)}, u32[]{:S(2)}) collective-permute-start(bf16[1,128,128]{2,1,0:T(8,128)(2,1)S(1)} %shard_map.94.after_ref.refs_4_), channel_id=1, source_target_pairs={{0,12},{4,8},{8,4},{12,0},{16,28},{20,24},{24,20},{28,16},{1,13},{... | collective-permute-start | bytes 98312 | tf_op jit(solution)/shard_map/ppermute | solution.py:32
  51.0 0.5 collective-permute-start.20
  51.5 1.2 %collective-permute-start.19 = (bf16[1,128,128]{2,1,0:T(8,128)(2,1)S(1)}, bf16[1,128,128]{2,1,0:T(8,128)(2,1)S(1)}, u32[]{:S(2)}, u32[]{:S(2)}) collective-permute-start(bf16[1,128,128]{2,1,0:T(8,128)(2,1)S(1)} %shard_map.94.after_ref.refs_4_), channel_id=1, source_target_pairs={{0,4},{4,0},{8,12},{12,8},{16,20},{20,16},{24,28},{28,24},{1,5},{5... | collective-permute-start | bytes 98312 | tf_op jit(solution)/shard_map/ppermute | solution.py:32
  52.7 1.8 %shard_map.95.refs_32_ = f32[4,240,512]{2,1,0:T(8,128)S(1)} custom-call(f32[4,4]{1,0:T(4,128)S(1)} %copy-done, bf16[240,512]{1,0:T(8,128)(2,1)S(1)} %get-tuple-element.68.q_ref.refs_12_, bf16[240,512]{1,0:T(8,128)(2,1)S(1)} %get-tuple-element.69.k_ref.refs_17_, bf16[240,512]{1,0:T(8,128)(2,1)S(1)} %get-tuple-element.70.v_ref.refs_22_, ...), custom_call_target="tpu_custom_call" | custom-call | flops 2949120000 | tf_op jit(solution)/shard_map/pallas_call | solution.py:40
  54.5 0.4 collective-permute-done.20.refs_6_
  54.9 0.5 collective-permute-done.19.refs_5_
  55.4 3.3 %shard_map.96 = (bf16[1024,512]{1,0:T(8,128)(2,1)}, bf16[1024,512]{1,0:T(8,128)(2,1)}, bf16[1024,512]{1,0:T(8,128)(2,1)}, bf16[1024,512]{1,0:T(8,128)(2,1)}) custom-call(f32[4,4]{1,0:T(4,128)S(1)} %copy-done, bf16[1024,512]{1,0:T(8,128)(2,1)S(1)} %get-tuple-element.39.g_ref, bf16[4,128,128]{2,1,0:T(8,128)(2,1)S(1)} %collective-permute-done.11.refs_0_.near_ref, ...), custom_call_target="tpu_custom_call" | custom-call | flops 1073741824 | tf_op jit(solution)/shard_map/pallas_call | solution.py:40
  (20 shorter events, 0.0 us)
Async XLA Ops:
  0.6 11.1 %collective-permute-start = (bf16[1024,512]{1,0:T(8,128)(2,1)}, bf16[1024,512]{1,0:T(8,128)(2,1)S(1)}, u32[]{:S(2)}, u32[]{:S(2)}) collective-permute-start(bf16[1024,512]{1,0:T(8,128)(2,1)} %refs_0_.4), channel_id=1, source_target_pairs={{0,1},{1,0},{2,3},{3,2},{4,5},{5,4},{6,7},{7,6},{8,9},{9,8},{10,11... | collective-permute-start | bytes 3145736 | tf_op jit(solution)/shard_map/ppermute | solution.py:32
  2.1 7.6 %collective-permute-start.5 = (bf16[160,512]{1,0:T(8,128)(2,1)S(1)}, bf16[160,512]{1,0:T(8,128)(2,1)S(1)}, u32[]{:S(2)}, u32[]{:S(2)}) collective-permute-start(bf16[160,512]{1,0:T(8,128)(2,1)S(1)} %shard_map.75.refs_1_.refs_0_), channel_id=1, source_target_pairs={{0,2},{1,3},{2,0},{3,1},{4,6},{5,7},{6,4},{7,5},{8,10},{9,11},{10,... | collective-permute-start | bytes 491528 | tf_op jit(solution)/shard_map/ppermute | solution.py:32
  6.0 8.0 %collective-permute-start.4 = (bf16[192,512]{1,0:T(8,128)(2,1)S(1)}, bf16[192,512]{1,0:T(8,128)(2,1)S(1)}, u32[]{:S(2)}, u32[]{:S(2)}) collective-permute-start(bf16[192,512]{1,0:T(8,128)(2,1)S(1)} %get-tuple-element.38.refs_2_.refs_0_), channel_id=1, source_target_pairs={{0,2},{1,3},{2,0},{3,1},{4,6},{5,7},{6,4},{7,5},{8,10},{9,11},{10,... | collective-permute-start | bytes 589832 | tf_op jit(solution)/shard_map/ppermute | solution.py:32
  9.7 2.0 %collective-permute-start.6 = (bf16[160,512]{1,0:T(8,128)(2,1)S(1)}, bf16[160,512]{1,0:T(8,128)(2,1)S(1)}, u32[]{:S(2)}, u32[]{:S(2)}) collective-permute-start(bf16[160,512]{1,0:T(8,128)(2,1)S(1)} %shard_map.78.refs_2_), channel_id=1, source_target_pairs={{0,1},{1,0},{2,3},{3,2},{4,5},{5,4},{6,7},{7,6},{8,9},{9,8},{10,11... | collective-permute-start | bytes 491528 | tf_op jit(solution)/shard_map/ppermute | solution.py:32
  9.7 9.4 %collective-permute-start.3 = (bf16[208,512]{1,0:T(8,128)(2,1)S(1)}, bf16[208,512]{1,0:T(8,128)(2,1)S(1)}, u32[]{:S(2)}, u32[]{:S(2)}) collective-permute-start(bf16[208,512]{1,0:T(8,128)(2,1)S(1)} %get-tuple-element.43.refs_0_), channel_id=1, source_target_pairs={{0,2},{1,3},{2,0},{3,1},{4,6},{5,7},{6,4},{7,5},{8,10},{9,11},{10,... | collective-permute-start | bytes 638984 | tf_op jit(solution)/shard_map/ppermute | solution.py:32
  11.7 4.2 %copy-start = (f32[4,4]{1,0:T(4,128)S(1)}, f32[4,4]{1,0:T(4,128)}, u32[]{:S(2)}) copy-start(f32[4,4]{1,0:T(4,128)} %weight_ref.11) | copy-start | bytes 196
  13.9 3.4 %collective-permute-start.7 = (bf16[192,512]{1,0:T(8,128)(2,1)S(1)}, bf16[192,512]{1,0:T(8,128)(2,1)S(1)}, u32[]{:S(2)}, u32[]{:S(2)}) collective-permute-start(bf16[192,512]{1,0:T(8,128)(2,1)S(1)} %shard_map.80.after_ref.refs_2_), channel_id=1, source_target_pairs={{0,1},{1,0},{2,3},{3,2},{4,5},{5,4},{6,7},{7,6},{8,9},{9,8},{10,11... | collective-permute-start | bytes 589832 | tf_op jit(solution)/shard_map/ppermute | solution.py:32
  13.9 9.9 %collective-permute-start.2 = (bf16[224,512]{1,0:T(8,128)(2,1)S(1)}, bf16[224,512]{1,0:T(8,128)(2,1)S(1)}, u32[]{:S(2)}, u32[]{:S(2)}) collective-permute-start(bf16[224,512]{1,0:T(8,128)(2,1)S(1)} %get-tuple-element.42.refs_0_), channel_id=1, source_target_pairs={{0,2},{1,3},{2,0},{3,1},{4,6},{5,7},{6,4},{7,5},{8,10},{9,11},{10,... | collective-permute-start | bytes 688136 | tf_op jit(solution)/shard_map/ppermute | solution.py:32
  19.1 2.9 %collective-permute-start.8 = (bf16[208,512]{1,0:T(8,128)(2,1)S(1)}, bf16[208,512]{1,0:T(8,128)(2,1)S(1)}, u32[]{:S(2)}, u32[]{:S(2)}) collective-permute-start(bf16[208,512]{1,0:T(8,128)(2,1)S(1)} %shard_map.83.after_ref.refs_2_), channel_id=1, source_target_pairs={{0,1},{1,0},{2,3},{3,2},{4,5},{5,4},{6,7},{7,6},{8,9},{9,8},{10,11... | collective-permute-start | bytes 638984 | tf_op jit(solution)/shard_map/ppermute | solution.py:32
  19.4 9.1 %collective-permute-start.1 = (bf16[240,512]{1,0:T(8,128)(2,1)S(1)}, bf16[240,512]{1,0:T(8,128)(2,1)S(1)}, u32[]{:S(2)}, u32[]{:S(2)}) collective-permute-start(bf16[240,512]{1,0:T(8,128)(2,1)S(1)} %get-tuple-element.41.refs_0_), channel_id=1, source_target_pairs={{0,2},{1,3},{2,0},{3,1},{4,6},{5,7},{6,4},{7,5},{8,10},{9,11},{10,... | collective-permute-start | bytes 737288 | tf_op jit(solution)/shard_map/ppermute | solution.py:32
  23.9 1.9 %collective-permute-start.9 = (bf16[224,512]{1,0:T(8,128)(2,1)S(1)}, bf16[224,512]{1,0:T(8,128)(2,1)S(1)}, u32[]{:S(2)}, u32[]{:S(2)}) collective-permute-start(bf16[224,512]{1,0:T(8,128)(2,1)S(1)} %shard_map.86.after_ref.refs_2_), channel_id=1, source_target_pairs={{0,1},{1,0},{2,3},{3,2},{4,5},{5,4},{6,7},{7,6},{8,9},{9,8},{10,11... | collective-permute-start | bytes 688136 | tf_op jit(solution)/shard_map/ppermute | solution.py:32
  28.5 1.5 %collective-permute-start.10 = (bf16[240,512]{1,0:T(8,128)(2,1)S(1)}, bf16[240,512]{1,0:T(8,128)(2,1)S(1)}, u32[]{:S(2)}, u32[]{:S(2)}) collective-permute-start(bf16[240,512]{1,0:T(8,128)(2,1)S(1)} %shard_map.89.refs_2_), channel_id=1, source_target_pairs={{0,1},{1,0},{2,3},{3,2},{4,5},{5,4},{6,7},{7,6},{8,9},{9,8},{10,11... | collective-permute-start | bytes 737288 | tf_op jit(solution)/shard_map/ppermute | solution.py:32
  30.9 7.0 %collective-permute-start.13 = (bf16[2,1,128,128]{3,2,1,0:T(8,128)(2,1)S(1)}, bf16[2,1,128,128]{3,2,1,0:T(8,128)(2,1)S(1)}, u32[]{:S(2)}, u32[]{:S(2)}) collective-permute-start(bf16[2,1,128,128]{3,2,1,0:T(8,128)(2,1)S(1)} %get-tuple-element.60), channel_id=1, source_target_pairs={{0,8},{4,12},{8,0},{12,4},{16,24},{20,28},{24,16},{28,20},{1,9},{5... | collective-permute-start | bytes 196616 | tf_op jit(solution)/shard_map/ppermute | solution.py:32
  32.8 5.2 %collective-permute-start.14 = (bf16[2,1,128,128]{3,2,1,0:T(8,128)(2,1)S(1)}, bf16[2,1,128,128]{3,2,1,0:T(8,128)(2,1)S(1)}, u32[]{:S(2)}, u32[]{:S(2)}) collective-permute-start(bf16[2,1,128,128]{3,2,1,0:T(8,128)(2,1)S(1)} %get-tuple-element.61), channel_id=1, source_target_pairs={{0,12},{4,8},{8,4},{12,0},{16,28},{20,24},{24,20},{28,16},{1,13},{... | collective-permute-start | bytes 196616 | tf_op jit(solution)/shard_map/ppermute | solution.py:32
  34.2 5.2 %collective-permute-start.12 = (bf16[2,1,128,128]{3,2,1,0:T(8,128)(2,1)S(1)}, bf16[2,1,128,128]{3,2,1,0:T(8,128)(2,1)S(1)}, u32[]{:S(2)}, u32[]{:S(2)}) collective-permute-start(bf16[2,1,128,128]{3,2,1,0:T(8,128)(2,1)S(1)} %get-tuple-element.59.after_ref), channel_id=1, source_target_pairs={{0,4},{4,0},{8,12},{12,8},{16,20},{20,16},{24,28},{28,24},{1,5},{5... | collective-permute-start | bytes 196616 | tf_op jit(solution)/shard_map/ppermute | solution.py:32
  34.5 14.7 %collective-permute-start.11 = (bf16[4,128,128]{2,1,0:T(8,128)(2,1)S(1)}, bf16[4,128,128]{2,1,0:T(8,128)(2,1)S(1)}, u32[]{:S(2)}, u32[]{:S(2)}) collective-permute-start(bf16[4,128,128]{2,1,0:T(8,128)(2,1)S(1)} %get-tuple-element.57), channel_id=1, source_target_pairs={{0,4},{4,0},{8,12},{12,8},{16,20},{20,16},{24,28},{28,24},{1,5},{5... | collective-permute-start | bytes 393224 | tf_op jit(solution)/shard_map/ppermute | solution.py:32
  40.0 6.1 %collective-permute-start.18 = (bf16[1,128,128]{2,1,0:T(8,128)(2,1)S(1)}, bf16[1,128,128]{2,1,0:T(8,128)(2,1)S(1)}, u32[]{:S(2)}, u32[]{:S(2)}) collective-permute-start(bf16[1,128,128]{2,1,0:T(8,128)(2,1)S(1)} %get-tuple-element.67), channel_id=1, source_target_pairs={{0,16},{4,20},{8,24},{12,28},{16,0},{20,4},{24,8},{28,12},{1,17},{... | collective-permute-start | bytes 98312 | tf_op jit(solution)/shard_map/ppermute | solution.py:32
  42.6 4.8 %collective-permute-start.17 = (bf16[1,128,128]{2,1,0:T(8,128)(2,1)S(1)}, bf16[1,128,128]{2,1,0:T(8,128)(2,1)S(1)}, u32[]{:S(2)}, u32[]{:S(2)}) collective-permute-start(bf16[1,128,128]{2,1,0:T(8,128)(2,1)S(1)} %get-tuple-element.66), channel_id=1, source_target_pairs={{0,12},{4,8},{8,4},{12,0},{16,28},{20,24},{24,20},{28,16},{1,13},{... | collective-permute-start | bytes 98312 | tf_op jit(solution)/shard_map/ppermute | solution.py:32
  44.1 3.9 %collective-permute-start.16 = (bf16[1,128,128]{2,1,0:T(8,128)(2,1)S(1)}, bf16[1,128,128]{2,1,0:T(8,128)(2,1)S(1)}, u32[]{:S(2)}, u32[]{:S(2)}) collective-permute-start(bf16[1,128,128]{2,1,0:T(8,128)(2,1)S(1)} %get-tuple-element.66), channel_id=1, source_target_pairs={{0,8},{4,12},{8,0},{12,4},{16,24},{20,28},{24,16},{28,20},{1,9},{5... | collective-permute-start | bytes 98312 | tf_op jit(solution)/shard_map/ppermute | solution.py:32
  45.3 3.9 %collective-permute-start.15 = (bf16[1,128,128]{2,1,0:T(8,128)(2,1)S(1)}, bf16[1,128,128]{2,1,0:T(8,128)(2,1)S(1)}, u32[]{:S(2)}, u32[]{:S(2)}) collective-permute-start(bf16[1,128,128]{2,1,0:T(8,128)(2,1)S(1)} %get-tuple-element.65.refs_1_.refs_0_), channel_id=1, source_target_pairs={{0,4},{4,0},{8,12},{12,8},{16,20},{20,16},{24,28},{28,24},{1,5},{5... | collective-permute-start | bytes 98312 | tf_op jit(solution)/shard_map/ppermute | solution.py:32
  49.2 5.3 %collective-permute-start.21 = (bf16[1,128,128]{2,1,0:T(8,128)(2,1)S(1)}, bf16[1,128,128]{2,1,0:T(8,128)(2,1)S(1)}, u32[]{:S(2)}, u32[]{:S(2)}) collective-permute-start(bf16[1,128,128]{2,1,0:T(8,128)(2,1)S(1)} %shard_map.94.after_ref.refs_4_), channel_id=1, source_target_pairs={{0,12},{4,8},{8,4},{12,0},{16,28},{20,24},{24,20},{28,16},{1,13},{... | collective-permute-start | bytes 98312 | tf_op jit(solution)/shard_map/ppermute | solution.py:32
  51.0 3.9 %collective-permute-start.20 = (bf16[1,128,128]{2,1,0:T(8,128)(2,1)S(1)}, bf16[1,128,128]{2,1,0:T(8,128)(2,1)S(1)}, u32[]{:S(2)}, u32[]{:S(2)}) collective-permute-start(bf16[1,128,128]{2,1,0:T(8,128)(2,1)S(1)} %shard_map.94.after_ref.refs_4_), channel_id=1, source_target_pairs={{0,8},{4,12},{8,0},{12,4},{16,24},{20,28},{24,16},{28,20},{1,9},{5... | collective-permute-start | bytes 98312 | tf_op jit(solution)/shard_map/ppermute | solution.py:32
  51.5 3.9 %collective-permute-start.19 = (bf16[1,128,128]{2,1,0:T(8,128)(2,1)S(1)}, bf16[1,128,128]{2,1,0:T(8,128)(2,1)S(1)}, u32[]{:S(2)}, u32[]{:S(2)}) collective-permute-start(bf16[1,128,128]{2,1,0:T(8,128)(2,1)S(1)} %shard_map.94.after_ref.refs_4_), channel_id=1, source_target_pairs={{0,4},{4,0},{8,12},{12,8},{16,20},{20,16},{24,28},{28,24},{1,5},{5... | collective-permute-start | bytes 98312 | tf_op jit(solution)/shard_map/ppermute | solution.py:32
where the time goes:
time: 59 us; the launch traced here: 58.8 us
  Pallas kernels  26.7 us (45%)
  starting transfers between devices  23.6 us (40%)
  waiting for transfers between devices  7.62 us (13%)
  between operations  0.98 us (2%)
    pallas_call x16, Pallas kernels, call(): pl.pallas_call(kernel, out_shape=outs, in_specs=specs, out_specs=[VMEM] *...  26.7 us
    ppermute x22, starting transfers between devices, swap(): return lax.ppermute(value, axis, pairs)  23.6 us
    ppermute x22, waiting for transfers between devices, swap(): return lax.ppermute(value, axis, pairs)  7.62 us
  transfers between devices with their start and end apart: 22, of which 11 were waited for; matrix products, arithmetic and copies ran while one was open for 0% of the time, Pallas kernels for 38%

commit v1 on v0

--- a/solution.py
+++ b/solution.py
@@ -312,14 +312,14 @@
 
     one = pltpu.VMEM((share, *square), BF16)
     got = [swap(send, "seq", m) for m, send in enumerate(sends, 1)]
-    near = swap(near, "seq", 1)
     fillers = [local(late[0], sends[0])]
+    near = swap(tie(near, fillers[0]), "seq", 1)
     mine, other, sums, sent = call(
         functools.partial(owner_kernel, last == 2),
         [one, one, running(2), message(2)],
         [totals, *got, fillers[0]],
         [VMEM] * GROUP + [ANY],
-        10**6,
+        5 * 10**9,
     )
     levels = spread(mine, other)
     for bit in range(2, last):
@@ -331,7 +331,7 @@
             10**6,
         )
         levels += spread(found, found)
-    found = tie(swap(sent, "seq", 1 << last), near, *levels)
+    found = tie(swap(sent, "seq", 1 << last), near)
     levels += spread(found, found)
     fillers += [local(c, found) for c in late[1:]]
     return near, levels, fillers

time: 59 us -> 55.7 us (0.944)
  waiting for transfers between devices: 7.62 us -> 4.06 us
    ppermute x22, waiting for transfers between devices: 7.62 us -> 4.06 us  [swap(): return lax.ppermute(value, axis, pairs)]
  transfers between devices with their start and end apart: 22 -> 22, of which waited for: 11 -> 6; matrix products, arithmetic and copies ran while one was open for 0% -> 0% of each run, Pallas kernels for 38% -> 40%
where the time goes in v1:
time: 55.7 us; the launch traced here: 55.5 us
  Pallas kernels  26.7 us (48%)
  starting transfers between devices  23.7 us (43%)
  waiting for transfers between devices  4.06 us (7%)
  between operations  1 us (2%)
    pallas_call x16, Pallas kernels, call(): pl.pallas_call(kernel, out_shape=outs, in_specs=specs, out_specs=[VMEM] *...  26.6 us
    ppermute x22, starting transfers between devices, swap(): return lax.ppermute(value, axis, pairs)  23.7 us
    ppermute x22, waiting for transfers between devices, swap(): return lax.ppermute(value, axis, pairs)  4.06 us
  transfers between devices with their start and end apart: 22, of which 6 were waited for; matrix products, arithmetic and copies ran while one was open for 0% of the time, Pallas kernels for 40%

profile of v1, /device:TPU:0, one launch (start us, length us, event | category | flops | bytes accessed | tf_op | source)
XLA Modules:
  0.0 55.5 jit_solution(4207538065505161670)
XLA Ops:
  0.6 0.5 collective-permute-start
  1.1 0.9 %shard_map.75.refs_1_.refs_0_ = bf16[160,512]{1,0:T(8,128)(2,1)S(1)} custom-call(bf16[1024,512]{1,0:T(8,128)(2,1)} %refs_0_.4), custom_call_target="tpu_custom_call" | custom-call | bytes 327680 | tf_op jit(solution)/shard_map/pallas_call | solution.py:40
  2.1 2.6 %collective-permute-start.5 = (bf16[160,512]{1,0:T(8,128)(2,1)S(1)}, bf16[160,512]{1,0:T(8,128)(2,1)S(1)}, u32[]{:S(2)}, u32[]{:S(2)}) collective-permute-start(bf16[160,512]{1,0:T(8,128)(2,1)S(1)} %shard_map.75.refs_1_.refs_0_), channel_id=1, source_target_pairs={{0,2},{1,3},{2,0},{3,1},{4,6},{5,7},{6,4},{7,5},{8,10},{9,11},{10,... | collective-permute-start | bytes 491528 | tf_op jit(solution)/shard_map/ppermute | solution.py:32
  4.7 1.3 %shard_map.76 = (bf16[192,512]{1,0:T(8,128)(2,1)S(1)}, bf16[208,512]{1,0:T(8,128)(2,1)S(1)}, bf16[224,512]{1,0:T(8,128)(2,1)S(1)}, bf16[240,512]{1,0:T(8,128)(2,1)S(1)}) custom-call(bf16[1024,512]{1,0:T(8,128)(2,1)} %refs_0_.4, bf16[160,512]{1,0:T(8,128)(2,1)S(1)} %shard_map.75.refs_1_.refs_0_), custom_call_target="tpu_custom_call" | custom-call | bytes 1769472 | tf_op jit(solution)/shard_map/pallas_call | solution.py:40
  6.0 0.1 collective-permute-start.4
  6.1 3.1 %shard_map.77 = (bf16[1024,512]{1,0:T(8,128)(2,1)S(1)}, bf16[3,2048,512]{2,1,0:T(8,128)(2,1)S(1)}) custom-call(bf16[1024,512]{1,0:T(8,128)(2,1)} %refs_0_.5, bf16[3,2048,512]{2,1,0:T(8,128)(2,1)} %refs_1_.1, bf16[192,512]{1,0:T(8,128)(2,1)S(1)} %get-tuple-element.38.refs_2_.refs_0_), custom_call_target="tpu_custom_call" | custom-call | bytes 14680064 | tf_op jit(solution)/shard_map/pallas_call | solution.py:40
  9.2 0.5 collective-permute-done.5.value_ref
  9.7 1.9 %collective-permute-start.3 = (bf16[208,512]{1,0:T(8,128)(2,1)S(1)}, bf16[208,512]{1,0:T(8,128)(2,1)S(1)}, u32[]{:S(2)}, u32[]{:S(2)}) collective-permute-start(bf16[208,512]{1,0:T(8,128)(2,1)S(1)} %get-tuple-element.43.refs_0_), channel_id=1, source_target_pairs={{0,2},{1,3},{2,0},{3,1},{4,6},{5,7},{6,4},{7,5},{8,10},{9,11},{10,... | collective-permute-start | bytes 638984 | tf_op jit(solution)/shard_map/ppermute | solution.py:32
  11.7 0.0 collective-permute-done.6.refs_3_
  11.7 0.0 collective-permute-done.refs_1_
  11.7 1.5 %shard_map.79 = (bf16[160,512]{1,0:T(8,128)(2,1)S(1)}, bf16[160,512]{1,0:T(8,128)(2,1)S(1)}, bf16[160,512]{1,0:T(8,128)(2,1)S(1)}, f32[2,4,128,128]{3,2,1,0:T(8,128)S(1)}) custom-call(bf16[3,2048,512]{2,1,0:T(8,128)(2,1)S(1)} %get-tuple-element.40.refs_0_.w_ref, bf16[1024,512]{1,0:T(8,128)(2,1)S(1)} %get-tuple-element.39.g_ref, ...), custom_call_target="tpu_custom_call" | custom-call | tf_op jit(solution)/shard_map/pallas_call | solution.py:40
  13.2 0.7 %collective-permute-done.4.value_ref = bf16[192,512]{1,0:T(8,128)(2,1)S(1)} collective-permute-done((bf16[192,512]{1,0:T(8,128)(2,1)S(1)}, bf16[192,512]{1,0:T(8,128)(2,1)S(1)}, u32[]{:S(2)}, u32[]{:S(2)}) %collective-permute-start.4) | collective-permute-done | bytes 196640 | tf_op jit(solution)/shard_map/ppermute | solution.py:32
  13.9 1.9 %collective-permute-start.2 = (bf16[224,512]{1,0:T(8,128)(2,1)S(1)}, bf16[224,512]{1,0:T(8,128)(2,1)S(1)}, u32[]{:S(2)}, u32[]{:S(2)}) collective-permute-start(bf16[224,512]{1,0:T(8,128)(2,1)S(1)} %get-tuple-element.42.refs_0_), channel_id=1, source_target_pairs={{0,2},{1,3},{2,0},{3,1},{4,6},{5,7},{6,4},{7,5},{8,10},{9,11},{10,... | collective-permute-start | bytes 688136 | tf_op jit(solution)/shard_map/ppermute | solution.py:32
  15.9 1.4 %shard_map.81.refs_4_.refs_28_ = f32[4,160,512]{2,1,0:T(8,128)S(1)} custom-call(f32[4,4]{1,0:T(4,128)S(1)} %copy-done, bf16[160,512]{1,0:T(8,128)(2,1)S(1)} %get-tuple-element.45.q_ref.refs_8_, bf16[160,512]{1,0:T(8,128)(2,1)S(1)} %get-tuple-element.46.k_ref.refs_13_, bf16[160,512]{1,0:T(8,128)(2,1)S(1)} %get-tuple-element.47.v_ref.refs_18_, ...), custom_call_target="tpu_custom_call" | custom-call | tf_op jit(solution)/shard_map/pallas_call | solution.py:40
  17.3 1.7 %shard_map.82 = (bf16[192,512]{1,0:T(8,128)(2,1)S(1)}, bf16[192,512]{1,0:T(8,128)(2,1)S(1)}, bf16[192,512]{1,0:T(8,128)(2,1)S(1)}, f32[2,4,128,128]{3,2,1,0:T(8,128)S(1)}) custom-call(bf16[3,2048,512]{2,1,0:T(8,128)(2,1)S(1)} %get-tuple-element.40.refs_0_.w_ref, bf16[1024,512]{1,0:T(8,128)(2,1)S(1)} %get-tuple-element.39.g_ref, ...), custom_call_target="tpu_custom_call" | custom-call | tf_op jit(solution)/shard_map/pallas_call | solution.py:40
  19.1 0.0 collective-permute-done.3.value_ref
  19.1 0.3 collective-permute-start.8
  19.4 1.1 %collective-permute-start.1 = (bf16[240,512]{1,0:T(8,128)(2,1)S(1)}, bf16[240,512]{1,0:T(8,128)(2,1)S(1)}, u32[]{:S(2)}, u32[]{:S(2)}) collective-permute-start(bf16[240,512]{1,0:T(8,128)(2,1)S(1)} %get-tuple-element.41.refs_0_), channel_id=1, source_target_pairs={{0,2},{1,3},{2,0},{3,1},{4,6},{5,7},{6,4},{7,5},{8,10},{9,11},{10,... | collective-permute-start | bytes 737288 | tf_op jit(solution)/shard_map/ppermute | solution.py:32
  20.5 1.6 %shard_map.84.refs_4_.refs_29_ = f32[4,192,512]{2,1,0:T(8,128)S(1)} custom-call(f32[4,4]{1,0:T(4,128)S(1)} %copy-done, bf16[192,512]{1,0:T(8,128)(2,1)S(1)} %get-tuple-element.49.q_ref.refs_9_, bf16[192,512]{1,0:T(8,128)(2,1)S(1)} %get-tuple-element.50.k_ref.refs_14_, bf16[192,512]{1,0:T(8,128)(2,1)S(1)} %get-tuple-element.51.v_ref.refs_19_, ...), custom_call_target="tpu_custom_call" | custom-call | tf_op jit(solution)/shard_map/pallas_call | solution.py:40
  22.1 1.8 %shard_map.85 = (bf16[208,512]{1,0:T(8,128)(2,1)S(1)}, bf16[208,512]{1,0:T(8,128)(2,1)S(1)}, bf16[208,512]{1,0:T(8,128)(2,1)S(1)}, f32[2,4,128,128]{3,2,1,0:T(8,128)S(1)}) custom-call(bf16[3,2048,512]{2,1,0:T(8,128)(2,1)S(1)} %get-tuple-element.40.refs_0_.w_ref, bf16[1024,512]{1,0:T(8,128)(2,1)S(1)} %get-tuple-element.39.g_ref, ...), custom_call_target="tpu_custom_call" | custom-call | tf_op jit(solution)/shard_map/pallas_call | solution.py:40
  23.9 0.3 collective-permute-start.9
  24.2 1.6 %shard_map.87.refs_4_.refs_30_ = f32[4,208,512]{2,1,0:T(8,128)S(1)} custom-call(f32[4,4]{1,0:T(4,128)S(1)} %copy-done, bf16[208,512]{1,0:T(8,128)(2,1)S(1)} %get-tuple-element.53.q_ref.refs_10_, bf16[208,512]{1,0:T(8,128)(2,1)S(1)} %get-tuple-element.54.k_ref.refs_15_, bf16[208,512]{1,0:T(8,128)(2,1)S(1)} %get-tuple-element.55.v_ref.refs_20_, ...), custom_call_target="tpu_custom_call" | custom-call | tf_op jit(solution)/shard_map/pallas_call | solution.py:40
  25.9 1.9 %shard_map.88 = (bf16[224,512]{1,0:T(8,128)(2,1)S(1)}, bf16[224,512]{1,0:T(8,128)(2,1)S(1)}, bf16[224,512]{1,0:T(8,128)(2,1)S(1)}, f32[2,4,128,128]{3,2,1,0:T(8,128)S(1)}) custom-call(bf16[3,2048,512]{2,1,0:T(8,128)(2,1)S(1)} %get-tuple-element.40.refs_0_.w_ref, bf16[1024,512]{1,0:T(8,128)(2,1)S(1)} %get-tuple-element.39.g_ref, ...), custom_call_target="tpu_custom_call" | custom-call | tf_op jit(solution)/shard_map/pallas_call | solution.py:40
  27.8 0.7 %collective-permute-done.1.value_ref = bf16[240,512]{1,0:T(8,128)(2,1)S(1)} collective-permute-done((bf16[240,512]{1,0:T(8,128)(2,1)S(1)}, bf16[240,512]{1,0:T(8,128)(2,1)S(1)}, u32[]{:S(2)}, u32[]{:S(2)}) %collective-permute-start.1) | collective-permute-done | bytes 245792 | tf_op jit(solution)/shard_map/ppermute | solution.py:32
  28.5 0.0 collective-permute-start.10
  28.5 1.3 %shard_map.90.part_ref = f32[3,240,512]{2,1,0:T(8,128)S(1)} custom-call(bf16[3,2048,512]{2,1,0:T(8,128)(2,1)S(1)} %get-tuple-element.40.refs_0_.w_ref, bf16[240,512]{1,0:T(8,128)(2,1)S(1)} %get-tuple-element.41.refs_0_, bf16[1024,512]{1,0:T(8,128)(2,1)S(1)} %collective-permute-done.refs_1_, bf16[240,512]{1,0:T(8,128)(2,1)S(1)} %shard_map.89.refs_2_), custom_call_target="tpu_custom_call" | custom-call | tf_op jit(solution)/shard_map/pallas_call | solution.py:40
  29.8 0.2 collective-permute-done.10.refs_0_
  30.0 0.9 %shard_map.91 = (bf16[240,512]{1,0:T(8,128)(2,1)S(1)}, bf16[240,512]{1,0:T(8,128)(2,1)S(1)}, bf16[240,512]{1,0:T(8,128)(2,1)S(1)}, f32[2,4,128,128]{3,2,1,0:T(8,...) custom-call(bf16[3,2048,512]{2,1,0:T(8,128)(2,1)S(1)} %get-tuple-ele, ...), custom_call_target="tpu_custom_call" | custom-call | tf_op jit(solution)/shard_map/pallas_call | solution.py:40
  30.9 1.9 %collective-permute-start.13 = (bf16[2,1,128,128]{3,2,1,0:T(8,128)(2,1)S(1)}, bf16[2,1,128,128]{3,2,1,0:T(8,128)(2,1)S(1)}, u32[]{:S(2)}, u32[]{:S(2)}) collective-permute-start(bf16[2,1,128,128]{3,2,1,0:T(8,128)(2,1)S(1)} %get-tuple-element.63), channel_id=1, source_target_pairs={{0,8},{4,12},{8,0},{12,4},{16,24},{20,28},{24,16},{28,20},{1,9},{5... | collective-permute-start | bytes 196616 | tf_op jit(solution)/shard_map/ppermute | solution.py:32
  32.8 1.4 %collective-permute-start.14 = (bf16[2,1,128,128]{3,2,1,0:T(8,128)(2,1)S(1)}, bf16[2,1,128,128]{3,2,1,0:T(8,128)(2,1)S(1)}, u32[]{:S(2)}, u32[]{:S(2)}) collective-permute-start(bf16[2,1,128,128]{3,2,1,0:T(8,128)(2,1)S(1)} %get-tuple-element.64), channel_id=1, source_target_pairs={{0,12},{4,8},{8,4},{12,0},{16,28},{20,24},{24,20},{28,16},{1,13},{... | collective-permute-start | bytes 196616 | tf_op jit(solution)/shard_map/ppermute | solution.py:32
  34.2 0.3 collective-permute-start.12
  34.5 1.7 %shard_map.92.refs_0_.refs_3_.refs_31_ = f32[4,224,512]{2,1,0:T(8,128)S(1)} custom-call(f32[4,4]{1,0:T(4,128)S(1)} %copy-done, bf16[224,512]{1,0:T(8,128)(2,1)S(1)} %get-tuple-element.58.q_ref.refs_11_, bf16[224,512]{1,0:T(8,128)(2,1)S(1)} %get-tuple-element.59.k_ref.refs_16_, bf16[224,512]{1,0:T(8,128)(2,1)S(1)} %get-tuple-element.60.v_ref.refs_21_, ...), custom_call_target="tpu_custom_call" | custom-call | flops 2569011200 | tf_op jit(solution)/shard_map/pallas_call | solution.py:40
  36.2 1.8 %collective-permute-start.11 = (bf16[4,128,128]{2,1,0:T(8,128)(2,1)S(1)}, bf16[4,128,128]{2,1,0:T(8,128)(2,1)S(1)}, u32[]{:S(2)}, u32[]{:S(2)}) collective-permute-start(bf16[4,128,128]{2,1,0:T(8,128)(2,1)S(1)} %shard_map.93), channel_id=1, source_target_pairs={{0,4},{4,0},{8,12},{12,8},{16,20},{20,16},{24,28},{28,24},{1,5},{5... | collective-permute-start | bytes 393224 | tf_op jit(solution)/shard_map/ppermute | solution.py:32
  38.0 0.0 collective-permute-done.13.refs_1_
  38.0 0.0 collective-permute-done.14.refs_2_
  38.0 1.4 %collective-permute-done.12.refs_0_ = bf16[2,1,128,128]{3,2,1,0:T(8,128)(2,1)S(1)} collective-permute-done((bf16[2,1,128,128]{3,2,1,0:T(8,128)(2,1)S(1)}, bf16[2,1,128,128]{3,2,1,0:T(8,128)(2,1)S(1)}, u32[]{:S(2)}, u32[]{:S(2)}) %collective-permute-start.12) | collective-permute-done | bytes 65568 | tf_op jit(solution)/shard_map/ppermute | solution.py:32
  39.4 0.6 %shard_map.94 = (bf16[1,128,128]{2,1,0:T(8,128)(2,1)S(1)}, bf16[1,128,128]{2,1,0:T(8,128)(2,1)S(1)}, f32[1,8,128]{2,1,0:T(8,128)}, bf16[1,128,128]{2,1,0:T(8,128)(2,1)S(1)}) custom-call(f32[2,4,128,128]{3,2,1,0:T(8,128)S(1)} %get-tuple-element.62.total_ref, bf16[2,1,128,128]{3,2,1,0:T(8,128)(2,1)S(1)} %collective-permute-done.12.refs_0_, ...), custom_call_target="tpu_custom_call" | custom-call | flops 5000000000 | tf_op jit(solution)/shard_map/pallas_call | solution.py:40
  40.0 2.6 %collective-permute-start.18 = (bf16[1,128,128]{2,1,0:T(8,128)(2,1)S(1)}, bf16[1,128,128]{2,1,0:T(8,128)(2,1)S(1)}, u32[]{:S(2)}, u32[]{:S(2)}) collective-permute-start(bf16[1,128,128]{2,1,0:T(8,128)(2,1)S(1)} %get-tuple-element.67), channel_id=1, source_target_pairs={{0,16},{4,20},{8,24},{12,28},{16,0},{20,4},{24,8},{28,12},{1,17},{... | collective-permute-start | bytes 98312 | tf_op jit(solution)/shard_map/ppermute | solution.py:32
  42.6 0.5 collective-permute-start.15
  43.1 2.5 %collective-permute-start.17 = (bf16[1,128,128]{2,1,0:T(8,128)(2,1)S(1)}, bf16[1,128,128]{2,1,0:T(8,128)(2,1)S(1)}, u32[]{:S(2)}, u32[]{:S(2)}) collective-permute-start(bf16[1,128,128]{2,1,0:T(8,128)(2,1)S(1)} %get-tuple-element.66), channel_id=1, source_target_pairs={{0,12},{4,8},{8,4},{12,0},{16,28},{20,24},{24,20},{28,16},{1,13},{... | collective-permute-start | bytes 98312 | tf_op jit(solution)/shard_map/ppermute | solution.py:32
  45.6 0.5 collective-permute-start.16
  46.1 0.0 collective-permute-done.18.value_ref
  46.1 1.3 %collective-permute-start.21 = (bf16[1,128,128]{2,1,0:T(8,128)(2,1)S(1)}, bf16[1,128,128]{2,1,0:T(8,128)(2,1)S(1)}, u32[]{:S(2)}, u32[]{:S(2)}) collective-permute-start(bf16[1,128,128]{2,1,0:T(8,128)(2,1)S(1)} %shard_map.95.after_ref.refs_4_), channel_id=1, source_target_pairs={{0,12},{4,8},{8,4},{12,0},{16,28},{20,24},{24,20},{28,16},{1,13},{... | collective-permute-start | bytes 98312 | tf_op jit(solution)/shard_map/ppermute | solution.py:32
  47.4 0.7 %collective-permute-start.20 = (bf16[1,128,128]{2,1,0:T(8,128)(2,1)S(1)}, bf16[1,128,128]{2,1,0:T(8,128)(2,1)S(1)}, u32[]{:S(2)}, u32[]{:S(2)}) collective-permute-start(bf16[1,128,128]{2,1,0:T(8,128)(2,1)S(1)} %shard_map.95.after_ref.refs_4_), channel_id=1, source_target_pairs={{0,8},{4,12},{8,0},{12,4},{16,24},{20,28},{24,16},{28,20},{1,9},{5... | collective-permute-start | bytes 98312 | tf_op jit(solution)/shard_map/ppermute | solution.py:32
  48.1 1.6 %collective-permute-start.19 = (bf16[1,128,128]{2,1,0:T(8,128)(2,1)S(1)}, bf16[1,128,128]{2,1,0:T(8,128)(2,1)S(1)}, u32[]{:S(2)}, u32[]{:S(2)}) collective-permute-start(bf16[1,128,128]{2,1,0:T(8,128)(2,1)S(1)} %shard_map.95.after_ref.refs_4_), channel_id=1, source_target_pairs={{0,4},{4,0},{8,12},{12,8},{16,20},{20,16},{24,28},{28,24},{1,5},{5... | collective-permute-start | bytes 98312 | tf_op jit(solution)/shard_map/ppermute | solution.py:32
  49.7 1.8 %shard_map.96.refs_32_ = f32[4,240,512]{2,1,0:T(8,128)S(1)} custom-call(f32[4,4]{1,0:T(4,128)S(1)} %copy-done, bf16[240,512]{1,0:T(8,128)(2,1)S(1)} %get-tuple-element.68.q_ref.refs_12_, bf16[240,512]{1,0:T(8,128)(2,1)S(1)} %get-tuple-element.69.k_ref.refs_17_, bf16[240,512]{1,0:T(8,128)(2,1)S(1)} %get-tuple-element.70.v_ref.refs_22_, ...), custom_call_target="tpu_custom_call" | custom-call | flops 2949120000 | tf_op jit(solution)/shard_map/pallas_call | solution.py:40
  51.5 0.5 collective-permute-done.19.refs_5_
  52.0 3.3 %shard_map.97 = (bf16[1024,512]{1,0:T(8,128)(2,1)}, bf16[1024,512]{1,0:T(8,128)(2,1)}, bf16[1024,512]{1,0:T(8,128)(2,1)}, bf16[1024,512]{1,0:T(8,128)(2,1)}) custom-call(f32[4,4]{1,0:T(4,128)S(1)} %copy-done, bf16[1024,512]{1,0:T(8,128)(2,1)S(1)} %get-tuple-element.39.g_ref, bf16[4,128,128]{2,1,0:T(8,128)(2,1)S(1)} %collective-permute-done.11.refs_0_.near_ref, ...), custom_call_target="tpu_custom_call" | custom-call | flops 1073741824 | tf_op jit(solution)/shard_map/pallas_call | solution.py:40
  (21 shorter events, 0.0 us)
Async XLA Ops:
  0.6 11.1 %collective-permute-start = (bf16[1024,512]{1,0:T(8,128)(2,1)}, bf16[1024,512]{1,0:T(8,128)(2,1)S(1)}, u32[]{:S(2)}, u32[]{:S(2)}) collective-permute-start(bf16[1024,512]{1,0:T(8,128)(2,1)} %refs_0_.4), channel_id=1, source_target_pairs={{0,1},{1,0},{2,3},{3,2},{4,5},{5,4},{6,7},{7,6},{8,9},{9,8},{10,11... | collective-permute-start | bytes 3145736 | tf_op jit(solution)/shard_map/ppermute | solution.py:32
  2.1 7.6 %collective-permute-start.5 = (bf16[160,512]{1,0:T(8,128)(2,1)S(1)}, bf16[160,512]{1,0:T(8,128)(2,1)S(1)}, u32[]{:S(2)}, u32[]{:S(2)}) collective-permute-start(bf16[160,512]{1,0:T(8,128)(2,1)S(1)} %shard_map.75.refs_1_.refs_0_), channel_id=1, source_target_pairs={{0,2},{1,3},{2,0},{3,1},{4,6},{5,7},{6,4},{7,5},{8,10},{9,11},{10,... | collective-permute-start | bytes 491528 | tf_op jit(solution)/shard_map/ppermute | solution.py:32
  6.0 8.0 %collective-permute-start.4 = (bf16[192,512]{1,0:T(8,128)(2,1)S(1)}, bf16[192,512]{1,0:T(8,128)(2,1)S(1)}, u32[]{:S(2)}, u32[]{:S(2)}) collective-permute-start(bf16[192,512]{1,0:T(8,128)(2,1)S(1)} %get-tuple-element.38.refs_2_.refs_0_), channel_id=1, source_target_pairs={{0,2},{1,3},{2,0},{3,1},{4,6},{5,7},{6,4},{7,5},{8,10},{9,11},{10,... | collective-permute-start | bytes 589832 | tf_op jit(solution)/shard_map/ppermute | solution.py:32
  9.7 2.0 %collective-permute-start.6 = (bf16[160,512]{1,0:T(8,128)(2,1)S(1)}, bf16[160,512]{1,0:T(8,128)(2,1)S(1)}, u32[]{:S(2)}, u32[]{:S(2)}) collective-permute-start(bf16[160,512]{1,0:T(8,128)(2,1)S(1)} %shard_map.78.refs_2_), channel_id=1, source_target_pairs={{0,1},{1,0},{2,3},{3,2},{4,5},{5,4},{6,7},{7,6},{8,9},{9,8},{10,11... | collective-permute-start | bytes 491528 | tf_op jit(solution)/shard_map/ppermute | solution.py:32
  9.7 9.4 %collective-permute-start.3 = (bf16[208,512]{1,0:T(8,128)(2,1)S(1)}, bf16[208,512]{1,0:T(8,128)(2,1)S(1)}, u32[]{:S(2)}, u32[]{:S(2)}) collective-permute-start(bf16[208,512]{1,0:T(8,128)(2,1)S(1)} %get-tuple-element.43.refs_0_), channel_id=1, source_target_pairs={{0,2},{1,3},{2,0},{3,1},{4,6},{5,7},{6,4},{7,5},{8,10},{9,11},{10,... | collective-permute-start | bytes 638984 | tf_op jit(solution)/shard_map/ppermute | solution.py:32
  11.7 4.2 %copy-start = (f32[4,4]{1,0:T(4,128)S(1)}, f32[4,4]{1,0:T(4,128)}, u32[]{:S(2)}) copy-start(f32[4,4]{1,0:T(4,128)} %weight_ref.11) | copy-start | bytes 196
  13.9 3.4 %collective-permute-start.7 = (bf16[192,512]{1,0:T(8,128)(2,1)S(1)}, bf16[192,512]{1,0:T(8,128)(2,1)S(1)}, u32[]{:S(2)}, u32[]{:S(2)}) collective-permute-start(bf16[192,512]{1,0:T(8,128)(2,1)S(1)} %shard_map.80.after_ref.refs_2_), channel_id=1, source_target_pairs={{0,1},{1,0},{2,3},{3,2},{4,5},{5,4},{6,7},{7,6},{8,9},{9,8},{10,11... | collective-permute-start | bytes 589832 | tf_op jit(solution)/shard_map/ppermute | solution.py:32
  13.9 9.9 %collective-permute-start.2 = (bf16[224,512]{1,0:T(8,128)(2,1)S(1)}, bf16[224,512]{1,0:T(8,128)(2,1)S(1)}, u32[]{:S(2)}, u32[]{:S(2)}) collective-permute-start(bf16[224,512]{1,0:T(8,128)(2,1)S(1)} %get-tuple-element.42.refs_0_), channel_id=1, source_target_pairs={{0,2},{1,3},{2,0},{3,1},{4,6},{5,7},{6,4},{7,5},{8,10},{9,11},{10,... | collective-permute-start | bytes 688136 | tf_op jit(solution)/shard_map/ppermute | solution.py:32
  19.1 2.9 %collective-permute-start.8 = (bf16[208,512]{1,0:T(8,128)(2,1)S(1)}, bf16[208,512]{1,0:T(8,128)(2,1)S(1)}, u32[]{:S(2)}, u32[]{:S(2)}) collective-permute-start(bf16[208,512]{1,0:T(8,128)(2,1)S(1)} %shard_map.83.after_ref.refs_2_), channel_id=1, source_target_pairs={{0,1},{1,0},{2,3},{3,2},{4,5},{5,4},{6,7},{7,6},{8,9},{9,8},{10,11... | collective-permute-start | bytes 638984 | tf_op jit(solution)/shard_map/ppermute | solution.py:32
  19.4 9.1 %collective-permute-start.1 = (bf16[240,512]{1,0:T(8,128)(2,1)S(1)}, bf16[240,512]{1,0:T(8,128)(2,1)S(1)}, u32[]{:S(2)}, u32[]{:S(2)}) collective-permute-start(bf16[240,512]{1,0:T(8,128)(2,1)S(1)} %get-tuple-element.41.refs_0_), channel_id=1, source_target_pairs={{0,2},{1,3},{2,0},{3,1},{4,6},{5,7},{6,4},{7,5},{8,10},{9,11},{10,... | collective-permute-start | bytes 737288 | tf_op jit(solution)/shard_map/ppermute | solution.py:32
  23.9 1.9 %collective-permute-start.9 = (bf16[224,512]{1,0:T(8,128)(2,1)S(1)}, bf16[224,512]{1,0:T(8,128)(2,1)S(1)}, u32[]{:S(2)}, u32[]{:S(2)}) collective-permute-start(bf16[224,512]{1,0:T(8,128)(2,1)S(1)} %shard_map.86.after_ref.refs_2_), channel_id=1, source_target_pairs={{0,1},{1,0},{2,3},{3,2},{4,5},{5,4},{6,7},{7,6},{8,9},{9,8},{10,11... | collective-permute-start | bytes 688136 | tf_op jit(solution)/shard_map/ppermute | solution.py:32
  28.5 1.5 %collective-permute-start.10 = (bf16[240,512]{1,0:T(8,128)(2,1)S(1)}, bf16[240,512]{1,0:T(8,128)(2,1)S(1)}, u32[]{:S(2)}, u32[]{:S(2)}) collective-permute-start(bf16[240,512]{1,0:T(8,128)(2,1)S(1)} %shard_map.89.refs_2_), channel_id=1, source_target_pairs={{0,1},{1,0},{2,3},{3,2},{4,5},{5,4},{6,7},{7,6},{8,9},{9,8},{10,11... | collective-permute-start | bytes 737288 | tf_op jit(solution)/shard_map/ppermute | solution.py:32
  30.9 7.1 %collective-permute-start.13 = (bf16[2,1,128,128]{3,2,1,0:T(8,128)(2,1)S(1)}, bf16[2,1,128,128]{3,2,1,0:T(8,128)(2,1)S(1)}, u32[]{:S(2)}, u32[]{:S(2)}) collective-permute-start(bf16[2,1,128,128]{3,2,1,0:T(8,128)(2,1)S(1)} %get-tuple-element.63), channel_id=1, source_target_pairs={{0,8},{4,12},{8,0},{12,4},{16,24},{20,28},{24,16},{28,20},{1,9},{5... | collective-permute-start | bytes 196616 | tf_op jit(solution)/shard_map/ppermute | solution.py:32
  32.8 5.2 %collective-permute-start.14 = (bf16[2,1,128,128]{3,2,1,0:T(8,128)(2,1)S(1)}, bf16[2,1,128,128]{3,2,1,0:T(8,128)(2,1)S(1)}, u32[]{:S(2)}, u32[]{:S(2)}) collective-permute-start(bf16[2,1,128,128]{3,2,1,0:T(8,128)(2,1)S(1)} %get-tuple-element.64), channel_id=1, source_target_pairs={{0,12},{4,8},{8,4},{12,0},{16,28},{20,24},{24,20},{28,16},{1,13},{... | collective-permute-start | bytes 196616 | tf_op jit(solution)/shard_map/ppermute | solution.py:32
  34.2 5.2 %collective-permute-start.12 = (bf16[2,1,128,128]{3,2,1,0:T(8,128)(2,1)S(1)}, bf16[2,1,128,128]{3,2,1,0:T(8,128)(2,1)S(1)}, u32[]{:S(2)}, u32[]{:S(2)}) collective-permute-start(bf16[2,1,128,128]{3,2,1,0:T(8,128)(2,1)S(1)} %get-tuple-element.61.after_ref), channel_id=1, source_target_pairs={{0,4},{4,0},{8,12},{12,8},{16,20},{20,16},{24,28},{28,24},{1,5},{5... | collective-permute-start | bytes 196616 | tf_op jit(solution)/shard_map/ppermute | solution.py:32
  36.2 9.9 %collective-permute-start.11 = (bf16[4,128,128]{2,1,0:T(8,128)(2,1)S(1)}, bf16[4,128,128]{2,1,0:T(8,128)(2,1)S(1)}, u32[]{:S(2)}, u32[]{:S(2)}) collective-permute-start(bf16[4,128,128]{2,1,0:T(8,128)(2,1)S(1)} %shard_map.93), channel_id=1, source_target_pairs={{0,4},{4,0},{8,12},{12,8},{16,20},{20,16},{24,28},{28,24},{1,5},{5... | collective-permute-start | bytes 393224 | tf_op jit(solution)/shard_map/ppermute | solution.py:32
  40.0 6.1 %collective-permute-start.18 = (bf16[1,128,128]{2,1,0:T(8,128)(2,1)S(1)}, bf16[1,128,128]{2,1,0:T(8,128)(2,1)S(1)}, u32[]{:S(2)}, u32[]{:S(2)}) collective-permute-start(bf16[1,128,128]{2,1,0:T(8,128)(2,1)S(1)} %get-tuple-element.67), channel_id=1, source_target_pairs={{0,16},{4,20},{8,24},{12,28},{16,0},{20,4},{24,8},{28,12},{1,17},{... | collective-permute-start | bytes 98312 | tf_op jit(solution)/shard_map/ppermute | solution.py:32
  42.6 5.5 %collective-permute-start.15 = (bf16[1,128,128]{2,1,0:T(8,128)(2,1)S(1)}, bf16[1,128,128]{2,1,0:T(8,128)(2,1)S(1)}, u32[]{:S(2)}, u32[]{:S(2)}) collective-permute-start(bf16[1,128,128]{2,1,0:T(8,128)(2,1)S(1)} %get-tuple-element.65.refs_0_), channel_id=1, source_target_pairs={{0,4},{4,0},{8,12},{12,8},{16,20},{20,16},{24,28},{28,24},{1,5},{5... | collective-permute-start | bytes 98312 | tf_op jit(solution)/shard_map/ppermute | solution.py:32
  43.1 8.4 %collective-permute-start.17 = (bf16[1,128,128]{2,1,0:T(8,128)(2,1)S(1)}, bf16[1,128,128]{2,1,0:T(8,128)(2,1)S(1)}, u32[]{:S(2)}, u32[]{:S(2)}) collective-permute-start(bf16[1,128,128]{2,1,0:T(8,128)(2,1)S(1)} %get-tuple-element.66), channel_id=1, source_target_pairs={{0,12},{4,8},{8,4},{12,0},{16,28},{20,24},{24,20},{28,16},{1,13},{... | collective-permute-start | bytes 98312 | tf_op jit(solution)/shard_map/ppermute | solution.py:32
  45.6 5.9 %collective-permute-start.16 = (bf16[1,128,128]{2,1,0:T(8,128)(2,1)S(1)}, bf16[1,128,128]{2,1,0:T(8,128)(2,1)S(1)}, u32[]{:S(2)}, u32[]{:S(2)}) collective-permute-start(bf16[1,128,128]{2,1,0:T(8,128)(2,1)S(1)} %get-tuple-element.66), channel_id=1, source_target_pairs={{0,8},{4,12},{8,0},{12,4},{16,24},{20,28},{24,16},{28,20},{1,9},{5... | collective-permute-start | bytes 98312 | tf_op jit(solution)/shard_map/ppermute | solution.py:32
  46.1 5.4 %collective-permute-start.21 = (bf16[1,128,128]{2,1,0:T(8,128)(2,1)S(1)}, bf16[1,128,128]{2,1,0:T(8,128)(2,1)S(1)}, u32[]{:S(2)}, u32[]{:S(2)}) collective-permute-start(bf16[1,128,128]{2,1,0:T(8,128)(2,1)S(1)} %shard_map.95.after_ref.refs_4_), channel_id=1, source_target_pairs={{0,12},{4,8},{8,4},{12,0},{16,28},{20,24},{24,20},{28,16},{1,13},{... | collective-permute-start | bytes 98312 | tf_op jit(solution)/shard_map/ppermute | solution.py:32
  47.4 4.1 %collective-permute-start.20 = (bf16[1,128,128]{2,1,0:T(8,128)(2,1)S(1)}, bf16[1,128,128]{2,1,0:T(8,128)(2,1)S(1)}, u32[]{:S(2)}, u32[]{:S(2)}) collective-permute-start(bf16[1,128,128]{2,1,0:T(8,128)(2,1)S(1)} %shard_map.95.after_ref.refs_4_), channel_id=1, source_target_pairs={{0,8},{4,12},{8,0},{12,4},{16,24},{20,28},{24,16},{28,20},{1,9},{5... | collective-permute-start | bytes 98312 | tf_op jit(solution)/shard_map/ppermute | solution.py:32
  48.1 3.9 %collective-permute-start.19 = (bf16[1,128,128]{2,1,0:T(8,128)(2,1)S(1)}, bf16[1,128,128]{2,1,0:T(8,128)(2,1)S(1)}, u32[]{:S(2)}, u32[]{:S(2)}) collective-permute-start(bf16[1,128,128]{2,1,0:T(8,128)(2,1)S(1)} %shard_map.95.after_ref.refs_4_), channel_id=1, source_target_pairs={{0,4},{4,0},{8,12},{12,8},{16,20},{20,16},{24,28},{28,24},{1,5},{5... | collective-permute-start | bytes 98312 | tf_op jit(solution)/shard_map/ppermute | solution.py:32

commit v2 on v1

--- a/solution.py
+++ b/solution.py
@@ -36,13 +36,14 @@
     return lax.rem(position // 2**bit, 2) == 1
 
 
-def call(kernel, outs, operands, specs, flops, scratch=(), out_specs=None, limit=4, moved=0):
+def call(kernel, outs, operands, specs, flops, scratch=(), out_specs=None, limit=4, moved=0, aliases=()):
     return pl.pallas_call(
         kernel,
         out_shape=outs,
         in_specs=specs,
         out_specs=[VMEM] * len(outs) if out_specs is None else out_specs,
         scratch_shapes=scratch,
+        input_output_aliases=dict(aliases),
         compiler_params=pltpu.CompilerParams(vmem_limit_bytes=limit * MIB),
         cost_estimate=pl.CostEstimate(flops=flops, bytes_accessed=moved, transcendentals=0),
     )(*operands)
@@ -235,64 +236,124 @@
     return jnp.concatenate([top, bottom], axis=0)
 
 
-def finish_kernel(spans, heads, groups, weight_ref, g_ref, near_ref, *refs):
+def gather_mixes(levels, first, side, weight_ref, block, mix_ref):
+    position = lax.axis_index("seq")
+    place = lax.rem(position, GROUP)
+    heads, size = mix_ref.shape[:2]
+    share = heads // GROUP
+    for m in range(GROUP):
+        for e in range(share):
+            h = (place ^ m) * share + e
+            total = None
+            for b in range(len(levels) // GROUP):
+                level = first + b
+                coef = weight_ref[h, level + 1] * (1.0 / math.sqrt(size * block * 2**level))
+                taken = bit_of(position, level)
+                if side == 1:
+                    taken = jnp.logical_not(taken)
+                term = jnp.where(taken, coef, 0.0) * levels[b * GROUP + m][e].astype(F32)
+                total = term if total is None else total + term
+            mix_ref[h] = total
+
+
+def write_side(spans, side, weight_of, q_refs, k_refs, v_refs, g_ref, part_refs, outs, held, sems):
     chunks = len(spans)
-    levels, refs = refs[: groups * GROUP], refs[groups * GROUP :]
+    size = held.shape[-1]
+    copies = []
+    for c in range(chunks) if side == 0 else reversed(range(chunks)):
+        span = slice(*spans[c])
+        weights = weight_of(c)
+        for j in range(2):
+            ref = (q_refs[c], g_ref, v_refs[c], k_refs[c])[2 * side + j]
+            rows = span if ref is g_ref else slice(None)
+            for p, weight in enumerate(weights):
+                cols = slice(p * weight.shape[0], (p + 1) * weight.shape[0])
+                term = dot(ref[rows, cols], weight, NT if 2 * side + j in (1, 2) else NN)
+                held[j, span, cols] = (term + part_refs[c][2 * side + j, :, cols]).astype(BF16)
+            copy = pltpu.make_async_copy(
+                held.at[j, span], outs[2 * side + j].at[span], sems.at[j, c]
+            )
+            copy.start()
+            copies.append(copy)
+    for copy in copies:
+        copy.wait()
+
+
+def early_side_kernel(spans, heads, top, weight_ref, g_ref, near_ref, *refs):
+    chunks = len(spans)
+    levels, refs = refs[: (top - 1) * GROUP], refs[(top - 1) * GROUP :]
     q_refs, refs = refs[:chunks], refs[chunks:]
     k_refs, refs = refs[:chunks], refs[chunks:]
     v_refs, refs = refs[:chunks], refs[chunks:]
     state_refs, refs = refs[:chunks], refs[chunks:]
     part_refs, refs = refs[:chunks], refs[chunks:]
-    outs, (held, mix_ref, sems) = refs[:4], refs[4:]
+    outs, (base_ref, held, mix_ref, sems) = refs[:4], refs[4:]
     position = lax.axis_index("seq")
-    place = lax.rem(position, GROUP)
-    size = q_refs[0].shape[1] // heads
-    share = heads // GROUP
     block = g_ref.shape[0]
+    size = mix_ref.shape[-1]
     norm = 1.0 / math.sqrt(size * block)
-    for m in range(GROUP):
-        for e in range(share):
-            h = (place ^ m) * share + e
-            values = [near_ref[h]] + [levels[b * GROUP + m][e] for b in range(groups)]
-            forward = backward = None
-            for level, value in enumerate(values):
-                coef = weight_ref[h, level + 1] * (1.0 / math.sqrt(size * block * 2**level))
-                on = bit_of(position, level)
-                value = value.astype(F32)
-                to_forward = jnp.where(on, coef, 0.0) * value
-                to_backward = jnp.where(on, 0.0, coef) * value
-                forward = to_forward if forward is None else forward + to_forward
-                backward = to_backward if backward is None else backward + to_backward
-            mix_ref[0, h] = forward
-            mix_ref[1, h] = backward
-    copies = []
-    for s in range(2):
-        sums = [mix_ref[s, h] for h in range(heads)]
-        for c in range(chunks) if s == 0 else reversed(range(chunks)):
-            span = slice(*spans[c])
-            weights = [pair_block(sums[h], sums[h + 1]) for h in range(0, heads, 2)]
-            for j in (2 * s, 2 * s + 1):
-                for h in range(0, heads, 2):
-                    cols = slice(h * size, (h + 2) * size)
-                    weight = weights[h // 2]
-                    if j == 0:
-                        term = dot(q_refs[c][:, cols], weight)
-                    elif j == 1:
-                        term = dot(g_ref[span, cols], weight, NT)
-                    elif j == 2:
-                        term = dot(v_refs[c][:, cols], weight, NT)
-                    else:
-                        term = dot(k_refs[c][:, cols], weight)
-                    held[j, span, cols] = (term + part_refs[c][j, :, cols]).astype(BF16)
-                copy = pltpu.make_async_copy(held.at[j, span], outs[j].at[span], sems.at[j, c])
-                copy.start()
-                copies.append(copy)
-            sums = [
-                total + weight_ref[h, 0] * norm * state_refs[c][s, h]
-                for h, total in enumerate(sums)
-            ]
-    for copy in copies:
-        copy.wait()
+
+    def sums_of(side):
+        gather_mixes(levels, 1, side, weight_ref, block, mix_ref)
+        taken = bit_of(position, 0)
+        if side == 1:
+            taken = jnp.logical_not(taken)
+        found = []
+        for h in range(heads):
+            coef = jnp.where(taken, weight_ref[h, 1] * norm, 0.0)
+            found.append(mix_ref[h] + coef * near_ref[h].astype(F32))
+        return found
+
+    def add(sums, side, c):
+        return [
+            total + weight_ref[h, 0] * norm * state_refs[c][side, h] for h, total in enumerate(sums)
+        ]
+
+    for side in range(2):
+        reached = bit_of(position, top)
+
+        @pl.when(reached if side == 1 else jnp.logical_not(reached))
+        def _():
+            sums = [sums_of(side)]
+
+            def weight_of(c):
+                weights = [pair_block(*sums[0][h : h + 2]) for h in range(0, heads, 2)]
+                sums[0] = add(sums[0], side, c)
+                return weights
+
+            write_side(
+                spans, side, weight_of, q_refs, k_refs, v_refs, g_ref, part_refs, outs, held, sems
+            )
+            other = sums_of(1 - side)
+            for c in range(chunks) if side == 1 else reversed(range(chunks)):
+                for h in range(heads):
+                    base_ref[c, h] = other[h]
+                other = add(other, 1 - side, c)
+
+
+def late_side_kernel(spans, heads, top, weight_ref, g_ref, base_ref, *refs):
+    chunks = len(spans)
+    levels, refs = refs[:GROUP], refs[GROUP:]
+    q_refs, refs = refs[:chunks], refs[chunks:]
+    k_refs, refs = refs[:chunks], refs[chunks:]
+    v_refs, refs = refs[:chunks], refs[chunks:]
+    part_refs, refs = refs[:chunks], refs[chunks:]
+    outs, (held, mix_ref, sems) = refs[-7:-3], refs[-3:]
+    block = g_ref.shape[0]
+    reached = bit_of(lax.axis_index("seq"), top)
+    for side in range(2):
+
+        @pl.when(reached if side == 0 else jnp.logical_not(reached))
+        def _():
+            gather_mixes(levels, top, side, weight_ref, block, mix_ref)
+
+            def weight_of(c):
+                sums = [base_ref[c, h] + mix_ref[h] for h in range(heads)]
+                return [pair_block(*sums[h : h + 2]) for h in range(0, heads, 2)]
+
+            write_side(
+                spans, side, weight_of, q_refs, k_refs, v_refs, g_ref, part_refs, outs, held, sems
+            )
 
 
 def exchange(totals, near, sends, local, late):
@@ -312,13 +373,13 @@
 
     one = pltpu.VMEM((share, *square), BF16)
     got = [swap(send, "seq", m) for m, send in enumerate(sends, 1)]
-    fillers = [local(late[0], sends[0])]
-    near = swap(tie(near, fillers[0]), "seq", 1)
+    fillers = [local(c, sends[0]) for c in late]
+    near = swap(tie(near, *fillers), "seq", 1)
     mine, other, sums, sent = call(
         functools.partial(owner_kernel, last == 2),
         [one, one, running(2), message(2)],
-        [totals, *got, fillers[0]],
-        [VMEM] * GROUP + [ANY],
+        [totals, *got, *fillers],
+        [VMEM] * GROUP + [ANY] * len(fillers),
         5 * 10**9,
     )
     levels = spread(mine, other)
@@ -333,7 +394,6 @@
         levels += spread(found, found)
     found = tie(swap(sent, "seq", 1 << last), near)
     levels += spread(found, found)
-    fillers += [local(c, found) for c in late[1:]]
     return near, levels, fillers
 
 
@@ -422,20 +482,36 @@
         after = got[3]
     near, levels, fillers = exchange(got[4], got[5], got[6:], local, range(len(locals_), CHUNKS))
     locals_ += fillers
-    operands = [level_weight, grads, near, *levels, *qs, *ks, *vs, *states, *locals_]
-    return call(
-        functools.partial(finish_kernel, spans, heads, len(levels) // GROUP),
-        [jax.ShapeDtypeStruct((rows, width), BF16)] * 4,
+    shapes = [jax.ShapeDtypeStruct((rows, width), BF16)] * 4
+    top = len(levels) // GROUP
+    flats = [*qs, *ks, *vs]
+    scratch = [
+        pltpu.VMEM((2, rows, width), BF16),
+        pltpu.VMEM((heads, size, size), F32),
+        pltpu.SemaphoreType.DMA((2, CHUNKS)),
+    ]
+    operands = [level_weight, grads, near, *levels[:-GROUP], *flats, *states, *locals_]
+    *written, base = call(
+        functools.partial(early_side_kernel, spans, heads, top),
+        [*shapes, pltpu.VMEM((CHUNKS, heads, size, size), F32)],
         operands,
         [SMEM] + [VMEM] * (len(operands) - 1),
-        16 * rows * size * width,
-        [
-            pltpu.VMEM((4, rows, width), BF16),
-            pltpu.VMEM((2, heads, size, size), F32),
-            pltpu.SemaphoreType.DMA((4, CHUNKS)),
-        ],
+        0,
+        scratch,
+        [ANY] * 4 + [VMEM],
+        8,
+    )
+    operands = [level_weight, grads, base, *levels[-GROUP:], *flats, *locals_]
+    return call(
+        functools.partial(late_side_kernel, spans, heads, top),
+        shapes,
+        [*operands, *written],
+        [SMEM] + [VMEM] * (len(operands) - 1) + [ANY] * 4,
+        0,
+        scratch,
         [ANY] * 4,
-        12,
+        8,
+        aliases={len(operands) + j: j for j in range(4)},
     )
 
 

time: 55.7 us -> 55.5 us (level)
  waiting for transfers between devices: 4.06 us -> 2.14 us
  Pallas kernels: 26.7 us -> 28.5 us
    ppermute x22, waiting for transfers between devices: 4.06 us -> 2.14 us  [swap(): return lax.ppermute(value, axis, pairs)]
    pallas_call x16 -> x17, Pallas kernels: 26.6 us -> 28.5 us  [call(): pl.pallas_call(kernel, out_shape=outs, in_specs=specs, out_specs=[VMEM] *...]
  transfers between devices with their start and end apart: 22 -> 22, of which waited for: 6 -> 4; matrix products, arithmetic and copies ran while one was open for 0% -> 0% of each run, Pallas kernels for 40% -> 46%
where the time goes in v2:
time: 55.5 us; the launch traced here: 55.3 us
  Pallas kernels  28.5 us (51%)
  starting transfers between devices  23.6 us (43%)
  waiting for transfers between devices  2.14 us (4%)
  between operations  1.01 us (2%)
    pallas_call x17, Pallas kernels, call(): pl.pallas_call(kernel, out_shape=outs, in_specs=specs, out_specs=[VMEM] *...  28.5 us
    ppermute x22, starting transfers between devices, swap(): return lax.ppermute(value, axis, pairs)  23.6 us
    ppermute x22, waiting for transfers between devices, swap(): return lax.ppermute(value, axis, pairs)  2.14 us
  transfers between devices with their start and end apart: 22, of which 4 were waited for; matrix products, arithmetic and copies ran while one was open for 0% of the time, Pallas kernels for 46%

profile of v2, /device:TPU:0, one launch (start us, length us, event | category | flops | bytes accessed | tf_op | source)
XLA Modules:
  0.0 55.3 jit_solution(6001950811294561237)
XLA Ops:
  0.6 0.5 collective-permute-start
  1.1 0.9 %shard_map.75.refs_1_.refs_0_ = bf16[160,512]{1,0:T(8,128)(2,1)S(1)} custom-call(bf16[1024,512]{1,0:T(8,128)(2,1)} %refs_0_.4), custom_call_target="tpu_custom_call" | custom-call | bytes 327680 | tf_op jit(solution)/shard_map/pallas_call | solution.py:40
  2.1 2.6 %collective-permute-start.5 = (bf16[160,512]{1,0:T(8,128)(2,1)S(1)}, bf16[160,512]{1,0:T(8,128)(2,1)S(1)}, u32[]{:S(2)}, u32[]{:S(2)}) collective-permute-start(bf16[160,512]{1,0:T(8,128)(2,1)S(1)} %shard_map.75.refs_1_.refs_0_), channel_id=1, source_target_pairs={{0,2},{1,3},{2,0},{3,1},{4,6},{5,7},{6,4},{7,5},{8,10},{9,11},{10,... | collective-permute-start | bytes 491528 | tf_op jit(solution)/shard_map/ppermute | solution.py:32
  4.7 1.3 %shard_map.76 = (bf16[192,512]{1,0:T(8,128)(2,1)S(1)}, bf16[208,512]{1,0:T(8,128)(2,1)S(1)}, bf16[224,512]{1,0:T(8,128)(2,1)S(1)}, bf16[240,512]{1,0:T(8,128)(2,1)S(1)}) custom-call(bf16[1024,512]{1,0:T(8,128)(2,1)} %refs_0_.4, bf16[160,512]{1,0:T(8,128)(2,1)S(1)} %shard_map.75.refs_1_.refs_0_), custom_call_target="tpu_custom_call" | custom-call | bytes 1769472 | tf_op jit(solution)/shard_map/pallas_call | solution.py:40
  6.0 0.1 collective-permute-start.4
  6.1 3.1 %shard_map.77 = (bf16[1024,512]{1,0:T(8,128)(2,1)S(1)}, bf16[3,2048,512]{2,1,0:T(8,128)(2,1)S(1)}) custom-call(bf16[1024,512]{1,0:T(8,128)(2,1)} %refs_0_.5, bf16[3,2048,512]{2,1,0:T(8,128)(2,1)} %refs_1_.1, bf16[192,512]{1,0:T(8,128)(2,1)S(1)} %get-tuple-element.43.refs_2_.refs_0_), custom_call_target="tpu_custom_call" | custom-call | bytes 14680064 | tf_op jit(solution)/shard_map/pallas_call | solution.py:40
  9.2 0.5 collective-permute-done.5.value_ref
  9.7 0.0 collective-permute-start.6
  9.7 1.9 %collective-permute-start.3 = (bf16[208,512]{1,0:T(8,128)(2,1)S(1)}, bf16[208,512]{1,0:T(8,128)(2,1)S(1)}, u32[]{:S(2)}, u32[]{:S(2)}) collective-permute-start(bf16[208,512]{1,0:T(8,128)(2,1)S(1)} %get-tuple-element.48.refs_0_), channel_id=1, source_target_pairs={{0,2},{1,3},{2,0},{3,1},{4,6},{5,7},{6,4},{7,5},{8,10},{9,11},{10,... | collective-permute-start | bytes 638984 | tf_op jit(solution)/shard_map/ppermute | solution.py:32
  11.7 1.5 %shard_map.79 = (bf16[160,512]{1,0:T(8,128)(2,1)S(1)}, bf16[160,512]{1,0:T(8,128)(2,1)S(1)}, bf16[160,512]{1,0:T(8,128)(2,1)S(1)}, f32[2,4,128,128]{3,2,1,0:T(8,128)S(1)}) custom-call(bf16[3,2048,512]{2,1,0:T(8,128)(2,1)S(1)} %get-tuple-element.45.refs_0_.w_ref, bf16[1024,512]{1,0:T(8,128)(2,1)S(1)} %get-tuple-element.44.g_ref, ...), custom_call_target="tpu_custom_call" | custom-call | tf_op jit(solution)/shard_map/pallas_call | solution.py:40
  13.2 0.7 %collective-permute-done.4.value_ref = bf16[192,512]{1,0:T(8,128)(2,1)S(1)} collective-permute-done((bf16[192,512]{1,0:T(8,128)(2,1)S(1)}, bf16[192,512]{1,0:T(8,128)(2,1)S(1)}, u32[]{:S(2)}, u32[]{:S(2)}) %collective-permute-start.4) | collective-permute-done | bytes 196640 | tf_op jit(solution)/shard_map/ppermute | solution.py:32
  13.9 0.0 collective-permute-start.7
  13.9 1.9 %collective-permute-start.2 = (bf16[224,512]{1,0:T(8,128)(2,1)S(1)}, bf16[224,512]{1,0:T(8,128)(2,1)S(1)}, u32[]{:S(2)}, u32[]{:S(2)}) collective-permute-start(bf16[224,512]{1,0:T(8,128)(2,1)S(1)} %get-tuple-element.47.refs_0_), channel_id=1, source_target_pairs={{0,2},{1,3},{2,0},{3,1},{4,6},{5,7},{6,4},{7,5},{8,10},{9,11},{10,... | collective-permute-start | bytes 688136 | tf_op jit(solution)/shard_map/ppermute | solution.py:32
  15.9 1.4 %shard_map.81.refs_4_.refs_24_.refs_19_ = f32[4,160,512]{2,1,0:T(8,128)S(1)} custom-call(f32[4,4]{1,0:T(4,128)S(1)} %copy-done, bf16[160,512]{1,0:T(8,128)(2,1)S(1)} %get-tuple-element.50.q_ref.refs_4_, bf16[160,512]{1,0:T(8,128)(2,1)S(1)} %get-tuple-element.51.k_ref.refs_9_, bf16[160,512]{1,0:T(8,128)(2,1)S(1)} %get-tuple-element.52.v_ref.refs_14_, ...), custom_call_target="tpu_custom_call" | custom-call | tf_op jit(solution)/shard_map/pallas_call | solution.py:40
  17.3 1.8 %shard_map.82 = (bf16[192,512]{1,0:T(8,128)(2,1)S(1)}, bf16[192,512]{1,0:T(8,128)(2,1)S(1)}, bf16[192,512]{1,0:T(8,128)(2,1)S(1)}, f32[2,4,128,128]{3,2,1,0:T(8,128)S(1)}) custom-call(bf16[3,2048,512]{2,1,0:T(8,128)(2,1)S(1)} %get-tuple-element.45.refs_0_.w_ref, bf16[1024,512]{1,0:T(8,128)(2,1)S(1)} %get-tuple-element.44.g_ref, ...), custom_call_target="tpu_custom_call" | custom-call | tf_op jit(solution)/shard_map/pallas_call | solution.py:40
  19.1 0.3 collective-permute-start.8
  19.4 1.0 %collective-permute-start.1 = (bf16[240,512]{1,0:T(8,128)(2,1)S(1)}, bf16[240,512]{1,0:T(8,128)(2,1)S(1)}, u32[]{:S(2)}, u32[]{:S(2)}) collective-permute-start(bf16[240,512]{1,0:T(8,128)(2,1)S(1)} %get-tuple-element.46.refs_0_), channel_id=1, source_target_pairs={{0,2},{1,3},{2,0},{3,1},{4,6},{5,7},{6,4},{7,5},{8,10},{9,11},{10,... | collective-permute-start | bytes 737288 | tf_op jit(solution)/shard_map/ppermute | solution.py:32
  20.5 1.6 %shard_map.84.refs_4_.refs_25_.refs_20_ = f32[4,192,512]{2,1,0:T(8,128)S(1)} custom-call(f32[4,4]{1,0:T(4,128)S(1)} %copy-done, bf16[192,512]{1,0:T(8,128)(2,1)S(1)} %get-tuple-element.54.q_ref.refs_5_, bf16[192,512]{1,0:T(8,128)(2,1)S(1)} %get-tuple-element.55.k_ref.refs_10_, bf16[192,512]{1,0:T(8,128)(2,1)S(1)} %get-tuple-element.56.v_ref.refs_15_, ...), custom_call_target="tpu_custom_call" | custom-call | tf_op jit(solution)/shard_map/pallas_call | solution.py:40
  22.0 0.0 collective-permute-done.8.refs_3_
  22.1 1.8 %shard_map.85 = (bf16[208,512]{1,0:T(8,128)(2,1)S(1)}, bf16[208,512]{1,0:T(8,128)(2,1)S(1)}, bf16[208,512]{1,0:T(8,128)(2,1)S(1)}, f32[2,4,128,128]{3,2,1,0:T(8,128)S(1)}) custom-call(bf16[3,2048,512]{2,1,0:T(8,128)(2,1)S(1)} %get-tuple-element.45.refs_0_.w_ref, bf16[1024,512]{1,0:T(8,128)(2,1)S(1)} %get-tuple-element.44.g_ref, ...), custom_call_target="tpu_custom_call" | custom-call | tf_op jit(solution)/shard_map/pallas_call | solution.py:40
  23.9 0.0 collective-permute-done.2.value_ref
  23.9 0.3 collective-permute-start.9
  24.2 1.7 %shard_map.87.refs_4_.refs_26_.refs_21_ = f32[4,208,512]{2,1,0:T(8,128)S(1)} custom-call(f32[4,4]{1,0:T(4,128)S(1)} %copy-done, bf16[208,512]{1,0:T(8,128)(2,1)S(1)} %get-tuple-element.58.q_ref.refs_6_, bf16[208,512]{1,0:T(8,128)(2,1)S(1)} %get-tuple-element.59.k_ref.refs_11_, bf16[208,512]{1,0:T(8,128)(2,1)S(1)} %get-tuple-element.60.v_ref.refs_16_, ...), custom_call_target="tpu_custom_call" | custom-call | tf_op jit(solution)/shard_map/pallas_call | solution.py:40
  25.9 1.9 %shard_map.88 = (bf16[224,512]{1,0:T(8,128)(2,1)S(1)}, bf16[224,512]{1,0:T(8,128)(2,1)S(1)}, bf16[224,512]{1,0:T(8,128)(2,1)S(1)}, f32[2,4,128,128]{3,2,1,0:T(8,128)S(1)}) custom-call(bf16[3,2048,512]{2,1,0:T(8,128)(2,1)S(1)} %get-tuple-element.45.refs_0_.w_ref, bf16[1024,512]{1,0:T(8,128)(2,1)S(1)} %get-tuple-element.44.g_ref, ...), custom_call_target="tpu_custom_call" | custom-call | tf_op jit(solution)/shard_map/pallas_call | solution.py:40
  27.8 0.7 %collective-permute-done.1.value_ref = bf16[240,512]{1,0:T(8,128)(2,1)S(1)} collective-permute-done((bf16[240,512]{1,0:T(8,128)(2,1)S(1)}, bf16[240,512]{1,0:T(8,128)(2,1)S(1)}, u32[]{:S(2)}, u32[]{:S(2)}) %collective-permute-start.1) | collective-permute-done | bytes 245792 | tf_op jit(solution)/shard_map/ppermute | solution.py:32
  28.5 1.3 %shard_map.90.part_ref = f32[3,240,512]{2,1,0:T(8,128)S(1)} custom-call(bf16[3,2048,512]{2,1,0:T(8,128)(2,1)S(1)} %get-tuple-element.45.refs_0_.w_ref, bf16[240,512]{1,0:T(8,128)(2,1)S(1)} %get-tuple-element.46.refs_0_, bf16[1024,512]{1,0:T(8,128)(2,1)S(1)} %collective-permute-done.refs_1_, bf16[240,512]{1,0:T(8,128)(2,1)S(1)} %shard_map.89.refs_2_), custom_call_target="tpu_custom_call" | custom-call | tf_op jit(solution)/shard_map/pallas_call | solution.py:40
  29.8 0.2 collective-permute-done.10.refs_0_
  30.0 0.9 %shard_map.91 = (bf16[240,512]{1,0:T(8,128)(2,1)S(1)}, bf16[240,512]{1,0:T(8,128)(2,1)S(1)}, bf16[240,512]{1,0:T(8,128)(2,1)S(1)}, f32[2,4,128,128]{3,2,1,0:T(8,...) custom-call(bf16[3,2048,512]{2,1,0:T(8,128)(2,1)S(1)} %get-tuple-ele, ...), custom_call_target="tpu_custom_call" | custom-call | tf_op jit(solution)/shard_map/pallas_call | solution.py:40
  30.9 1.9 %collective-permute-start.13 = (bf16[2,1,128,128]{3,2,1,0:T(8,128)(2,1)S(1)}, bf16[2,1,128,128]{3,2,1,0:T(8,128)(2,1)S(1)}, u32[]{:S(2)}, u32[]{:S(2)}) collective-permute-start(bf16[2,1,128,128]{3,2,1,0:T(8,128)(2,1)S(1)} %get-tuple-element.71), channel_id=1, source_target_pairs={{0,8},{4,12},{8,0},{12,4},{16,24},{20,28},{24,16},{28,20},{1,9},{5... | collective-permute-start | bytes 196616 | tf_op jit(solution)/shard_map/ppermute | solution.py:32
  32.8 1.4 %collective-permute-start.14 = (bf16[2,1,128,128]{3,2,1,0:T(8,128)(2,1)S(1)}, bf16[2,1,128,128]{3,2,1,0:T(8,128)(2,1)S(1)}, u32[]{:S(2)}, u32[]{:S(2)}) collective-permute-start(bf16[2,1,128,128]{3,2,1,0:T(8,128)(2,1)S(1)} %get-tuple-element.72), channel_id=1, source_target_pairs={{0,12},{4,8},{8,4},{12,0},{16,28},{20,24},{24,20},{28,16},{1,13},{... | collective-permute-start | bytes 196616 | tf_op jit(solution)/shard_map/ppermute | solution.py:32
  34.2 0.3 collective-permute-start.12
  34.5 1.8 %shard_map.93.refs_1_.refs_4_.refs_28_.refs_23_ = f32[4,240,512]{2,1,0:T(8,128)S(1)} custom-call(f32[4,4]{1,0:T(4,128)S(1)} %copy-done, bf16[240,512]{1,0:T(8,128)(2,1)S(1)} %get-tuple-element.67.q_ref.refs_8_, bf16[240,512]{1,0:T(8,128)(2,1)S(1)} %get-tuple-element.68.k_ref.refs_13_, bf16[240,512]{1,0:T(8,128)(2,1)S(1)} %get-tuple-element.69.v_ref.refs_18_, ...), custom_call_target="tpu_custom_call" | custom-call | flops 2949120000 | tf_op jit(solution)/shard_map/pallas_call | solution.py:40
  36.3 1.9 %shard_map.92.refs_0_.refs_3_.refs_27_.refs_22_ = f32[4,224,512]{2,1,0:T(8,128)S(1)} custom-call(f32[4,4]{1,0:T(4,128)S(1)} %copy-done, bf16[224,512]{1,0:T(8,128)(2,1)S(1)} %get-tuple-element.63.q_ref.refs_7_, bf16[224,512]{1,0:T(8,128)(2,1)S(1)} %get-tuple-element.64.k_ref.refs_12_, bf16[224,512]{1,0:T(8,128)(2,1)S(1)} %get-tuple-element.65.v_ref.refs_17_, ...), custom_call_target="tpu_custom_call" | custom-call | flops 2569011200 | tf_op jit(solution)/shard_map/pallas_call | solution.py:40
  38.2 1.8 %collective-permute-start.11 = (bf16[4,128,128]{2,1,0:T(8,128)(2,1)S(1)}, bf16[4,128,128]{2,1,0:T(8,128)(2,1)S(1)}, u32[]{:S(2)}, u32[]{:S(2)}) collective-permute-start(bf16[4,128,128]{2,1,0:T(8,128)(2,1)S(1)} %shard_map.94), channel_id=1, source_target_pairs={{0,4},{4,0},{8,12},{12,8},{16,20},{20,16},{24,28},{28,24},{1,5},{5... | collective-permute-start | bytes 393224 | tf_op jit(solution)/shard_map/ppermute | solution.py:32
  40.0 0.0 collective-permute-done.13.refs_1_
  40.0 0.0 collective-permute-done.14.refs_2_
  40.0 0.0 collective-permute-done.12.refs_0_
  40.0 0.6 %shard_map.95 = (bf16[1,128,128]{2,1,0:T(8,128)(2,1)S(1)}, bf16[1,128,128]{2,1,0:T(8,128)(2,1)S(1)}, f32[1,8,128]{2,1,0:T(8,128)}, bf16[1,128,128]{2,1,0:T(8,128)(2,1)S(1)}) custom-call(f32[2,4,128,128]{3,2,1,0:T(8,128)S(1)} %get-tuple-element.70.total_ref, bf16[2,1,128,128]{3,2,1,0:T(8,128)(2,1)S(1)} %collective-permute-done.12.refs_0_, ...), custom_call_target="tpu_custom_call" | custom-call | flops 5000000000 | tf_op jit(solution)/shard_map/pallas_call | solution.py:40
  40.6 2.6 %collective-permute-start.18 = (bf16[1,128,128]{2,1,0:T(8,128)(2,1)S(1)}, bf16[1,128,128]{2,1,0:T(8,128)(2,1)S(1)}, u32[]{:S(2)}, u32[]{:S(2)}) collective-permute-start(bf16[1,128,128]{2,1,0:T(8,128)(2,1)S(1)} %get-tuple-element.77), channel_id=1, source_target_pairs={{0,16},{4,20},{8,24},{12,28},{16,0},{20,4},{24,8},{28,12},{1,17},{... | collective-permute-start | bytes 98312 | tf_op jit(solution)/shard_map/ppermute | solution.py:32
  43.2 0.5 collective-permute-start.15
  43.7 2.5 %collective-permute-start.17 = (bf16[1,128,128]{2,1,0:T(8,128)(2,1)S(1)}, bf16[1,128,128]{2,1,0:T(8,128)(2,1)S(1)}, u32[]{:S(2)}, u32[]{:S(2)}) collective-permute-start(bf16[1,128,128]{2,1,0:T(8,128)(2,1)S(1)} %get-tuple-element.74), channel_id=1, source_target_pairs={{0,12},{4,8},{8,4},{12,0},{16,28},{20,24},{24,20},{28,16},{1,13},{... | collective-permute-start | bytes 98312 | tf_op jit(solution)/shard_map/ppermute | solution.py:32
  46.2 0.5 collective-permute-start.16
  46.7 0.0 collective-permute-done.18.value_ref
  46.7 1.5 %collective-permute-start.21 = (bf16[1,128,128]{2,1,0:T(8,128)(2,1)S(1)}, bf16[1,128,128]{2,1,0:T(8,128)(2,1)S(1)}, u32[]{:S(2)}, u32[]{:S(2)}) collective-permute-start(bf16[1,128,128]{2,1,0:T(8,128)(2,1)S(1)} %shard_map.97.refs_0_), channel_id=1, source_target_pairs={{0,12},{4,8},{8,4},{12,0},{16,28},{20,24},{24,20},{28,16},{1,13},{... | collective-permute-start | bytes 98312 | tf_op jit(solution)/shard_map/ppermute | solution.py:32
  48.3 0.4 collective-permute-start.20
  48.7 1.5 %collective-permute-start.19 = (bf16[1,128,128]{2,1,0:T(8,128)(2,1)S(1)}, bf16[1,128,128]{2,1,0:T(8,128)(2,1)S(1)}, u32[]{:S(2)}, u32[]{:S(2)}) collective-permute-start(bf16[1,128,128]{2,1,0:T(8,128)(2,1)S(1)} %shard_map.97.refs_0_), channel_id=1, source_target_pairs={{0,4},{4,0},{8,12},{12,8},{16,20},{20,16},{24,28},{28,24},{1,5},{5... | collective-permute-start | bytes 98312 | tf_op jit(solution)/shard_map/ppermute | solution.py:32
  50.2 2.5 %shard_map.96 = (bf16[1024,512]{1,0:T(8,128)(2,1)}, bf16[1024,512]{1,0:T(8,128)(2,1)}, bf16[1024,512]{1,0:T(8,128)(2,1)}, bf16[1024,512]{1,0:T(8,128)(2,1)}, f32[5,4,128,128]{3,2,1,0:T(8,128)S(1)}) custom-call(f32[4,4]{1,0:T(4,128)S(1)} %copy-done, bf16[1024,512]{1,0:T(8,128)(2,1)S(1)} %get-tuple-element.44.g_ref, ...), custom_call_target="tpu_custom_call" | custom-call | tf_op jit(solution)/shard_map/pallas_call | solution.py:40
  52.8 2.4 %shard_map.98 = (bf16[1024,512]{1,0:T(8,128)(2,1)}, bf16[1024,512]{1,0:T(8,128)(2,1)}, bf16[1024,512]{1,0:T(8,128)(2,1)}, bf16[1024,512]{1,0:T(8,128)(2,1)}) custom-call(f32[4,4]{1,0:T(4,128)S(1)} %copy-done, bf16[1024,512]{1,0:T(8,128)(2,1)S(1)} %get-tuple-element.44.g_ref, ...), custom_call_target="tpu_custom_call", output_to_operand_aliasing={{0}: (27, {}), {1}: (28, {}), {2}: (29, {}), {3}: (30, {})} | custom-call | tf_op jit(solution)/shard_map/pallas_call | solution.py:40
  (22 shorter events, 0.0 us)
Async XLA Ops:
  0.6 11.1 %collective-permute-start = (bf16[1024,512]{1,0:T(8,128)(2,1)}, bf16[1024,512]{1,0:T(8,128)(2,1)S(1)}, u32[]{:S(2)}, u32[]{:S(2)}) collective-permute-start(bf16[1024,512]{1,0:T(8,128)(2,1)} %refs_0_.4), channel_id=1, source_target_pairs={{0,1},{1,0},{2,3},{3,2},{4,5},{5,4},{6,7},{7,6},{8,9},{9,8},{10,11... | collective-permute-start | bytes 3145736 | tf_op jit(solution)/shard_map/ppermute | solution.py:32
  2.1 7.6 %collective-permute-start.5 = (bf16[160,512]{1,0:T(8,128)(2,1)S(1)}, bf16[160,512]{1,0:T(8,128)(2,1)S(1)}, u32[]{:S(2)}, u32[]{:S(2)}) collective-permute-start(bf16[160,512]{1,0:T(8,128)(2,1)S(1)} %shard_map.75.refs_1_.refs_0_), channel_id=1, source_target_pairs={{0,2},{1,3},{2,0},{3,1},{4,6},{5,7},{6,4},{7,5},{8,10},{9,11},{10,... | collective-permute-start | bytes 491528 | tf_op jit(solution)/shard_map/ppermute | solution.py:32
  6.0 8.0 %collective-permute-start.4 = (bf16[192,512]{1,0:T(8,128)(2,1)S(1)}, bf16[192,512]{1,0:T(8,128)(2,1)S(1)}, u32[]{:S(2)}, u32[]{:S(2)}) collective-permute-start(bf16[192,512]{1,0:T(8,128)(2,1)S(1)} %get-tuple-element.43.refs_2_.refs_0_), channel_id=1, source_target_pairs={{0,2},{1,3},{2,0},{3,1},{4,6},{5,7},{6,4},{7,5},{8,10},{9,11},{10,... | collective-permute-start | bytes 589832 | tf_op jit(solution)/shard_map/ppermute | solution.py:32
  9.7 2.0 %collective-permute-start.6 = (bf16[160,512]{1,0:T(8,128)(2,1)S(1)}, bf16[160,512]{1,0:T(8,128)(2,1)S(1)}, u32[]{:S(2)}, u32[]{:S(2)}) collective-permute-start(bf16[160,512]{1,0:T(8,128)(2,1)S(1)} %shard_map.78.refs_2_), channel_id=1, source_target_pairs={{0,1},{1,0},{2,3},{3,2},{4,5},{5,4},{6,7},{7,6},{8,9},{9,8},{10,11... | collective-permute-start | bytes 491528 | tf_op jit(solution)/shard_map/ppermute | solution.py:32
  9.7 9.4 %collective-permute-start.3 = (bf16[208,512]{1,0:T(8,128)(2,1)S(1)}, bf16[208,512]{1,0:T(8,128)(2,1)S(1)}, u32[]{:S(2)}, u32[]{:S(2)}) collective-permute-start(bf16[208,512]{1,0:T(8,128)(2,1)S(1)} %get-tuple-element.48.refs_0_), channel_id=1, source_target_pairs={{0,2},{1,3},{2,0},{3,1},{4,6},{5,7},{6,4},{7,5},{8,10},{9,11},{10,... | collective-permute-start | bytes 638984 | tf_op jit(solution)/shard_map/ppermute | solution.py:32
  11.7 4.2 %copy-start = (f32[4,4]{1,0:T(4,128)S(1)}, f32[4,4]{1,0:T(4,128)}, u32[]{:S(2)}) copy-start(f32[4,4]{1,0:T(4,128)} %weight_ref.13) | copy-start | bytes 196
  13.9 3.4 %collective-permute-start.7 = (bf16[192,512]{1,0:T(8,128)(2,1)S(1)}, bf16[192,512]{1,0:T(8,128)(2,1)S(1)}, u32[]{:S(2)}, u32[]{:S(2)}) collective-permute-start(bf16[192,512]{1,0:T(8,128)(2,1)S(1)} %shard_map.80.after_ref.refs_2_), channel_id=1, source_target_pairs={{0,1},{1,0},{2,3},{3,2},{4,5},{5,4},{6,7},{7,6},{8,9},{9,8},{10,11... | collective-permute-start | bytes 589832 | tf_op jit(solution)/shard_map/ppermute | solution.py:32
  13.9 9.9 %collective-permute-start.2 = (bf16[224,512]{1,0:T(8,128)(2,1)S(1)}, bf16[224,512]{1,0:T(8,128)(2,1)S(1)}, u32[]{:S(2)}, u32[]{:S(2)}) collective-permute-start(bf16[224,512]{1,0:T(8,128)(2,1)S(1)} %get-tuple-element.47.refs_0_), channel_id=1, source_target_pairs={{0,2},{1,3},{2,0},{3,1},{4,6},{5,7},{6,4},{7,5},{8,10},{9,11},{10,... | collective-permute-start | bytes 688136 | tf_op jit(solution)/shard_map/ppermute | solution.py:32
  19.1 2.9 %collective-permute-start.8 = (bf16[208,512]{1,0:T(8,128)(2,1)S(1)}, bf16[208,512]{1,0:T(8,128)(2,1)S(1)}, u32[]{:S(2)}, u32[]{:S(2)}) collective-permute-start(bf16[208,512]{1,0:T(8,128)(2,1)S(1)} %shard_map.83.after_ref.refs_2_), channel_id=1, source_target_pairs={{0,1},{1,0},{2,3},{3,2},{4,5},{5,4},{6,7},{7,6},{8,9},{9,8},{10,11... | collective-permute-start | bytes 638984 | tf_op jit(solution)/shard_map/ppermute | solution.py:32
  19.4 9.1 %collective-permute-start.1 = (bf16[240,512]{1,0:T(8,128)(2,1)S(1)}, bf16[240,512]{1,0:T(8,128)(2,1)S(1)}, u32[]{:S(2)}, u32[]{:S(2)}) collective-permute-start(bf16[240,512]{1,0:T(8,128)(2,1)S(1)} %get-tuple-element.46.refs_0_), channel_id=1, source_target_pairs={{0,2},{1,3},{2,0},{3,1},{4,6},{5,7},{6,4},{7,5},{8,10},{9,11},{10,... | collective-permute-start | bytes 737288 | tf_op jit(solution)/shard_map/ppermute | solution.py:32
  23.9 1.9 %collective-permute-start.9 = (bf16[224,512]{1,0:T(8,128)(2,1)S(1)}, bf16[224,512]{1,0:T(8,128)(2,1)S(1)}, u32[]{:S(2)}, u32[]{:S(2)}) collective-permute-start(bf16[224,512]{1,0:T(8,128)(2,1)S(1)} %shard_map.86.after_ref.refs_2_), channel_id=1, source_target_pairs={{0,1},{1,0},{2,3},{3,2},{4,5},{5,4},{6,7},{7,6},{8,9},{9,8},{10,11... | collective-permute-start | bytes 688136 | tf_op jit(solution)/shard_map/ppermute | solution.py:32
  28.5 1.5 %collective-permute-start.10 = (bf16[240,512]{1,0:T(8,128)(2,1)S(1)}, bf16[240,512]{1,0:T(8,128)(2,1)S(1)}, u32[]{:S(2)}, u32[]{:S(2)}) collective-permute-start(bf16[240,512]{1,0:T(8,128)(2,1)S(1)} %shard_map.89.refs_2_), channel_id=1, source_target_pairs={{0,1},{1,0},{2,3},{3,2},{4,5},{5,4},{6,7},{7,6},{8,9},{9,8},{10,11... | collective-permute-start | bytes 737288 | tf_op jit(solution)/shard_map/ppermute | solution.py:32
  30.9 9.1 %collective-permute-start.13 = (bf16[2,1,128,128]{3,2,1,0:T(8,128)(2,1)S(1)}, bf16[2,1,128,128]{3,2,1,0:T(8,128)(2,1)S(1)}, u32[]{:S(2)}, u32[]{:S(2)}) collective-permute-start(bf16[2,1,128,128]{3,2,1,0:T(8,128)(2,1)S(1)} %get-tuple-element.71), channel_id=1, source_target_pairs={{0,8},{4,12},{8,0},{12,4},{16,24},{20,28},{24,16},{28,20},{1,9},{5... | collective-permute-start | bytes 196616 | tf_op jit(solution)/shard_map/ppermute | solution.py:32
  32.8 7.2 %collective-permute-start.14 = (bf16[2,1,128,128]{3,2,1,0:T(8,128)(2,1)S(1)}, bf16[2,1,128,128]{3,2,1,0:T(8,128)(2,1)S(1)}, u32[]{:S(2)}, u32[]{:S(2)}) collective-permute-start(bf16[2,1,128,128]{3,2,1,0:T(8,128)(2,1)S(1)} %get-tuple-element.72), channel_id=1, source_target_pairs={{0,12},{4,8},{8,4},{12,0},{16,28},{20,24},{24,20},{28,16},{1,13},{... | collective-permute-start | bytes 196616 | tf_op jit(solution)/shard_map/ppermute | solution.py:32
  34.2 5.8 %collective-permute-start.12 = (bf16[2,1,128,128]{3,2,1,0:T(8,128)(2,1)S(1)}, bf16[2,1,128,128]{3,2,1,0:T(8,128)(2,1)S(1)}, u32[]{:S(2)}, u32[]{:S(2)}) collective-permute-start(bf16[2,1,128,128]{3,2,1,0:T(8,128)(2,1)S(1)} %get-tuple-element.66.after_ref), channel_id=1, source_target_pairs={{0,4},{4,0},{8,12},{12,8},{16,20},{20,16},{24,28},{28,24},{1,5},{5... | collective-permute-start | bytes 196616 | tf_op jit(solution)/shard_map/ppermute | solution.py:32
  38.2 8.5 %collective-permute-start.11 = (bf16[4,128,128]{2,1,0:T(8,128)(2,1)S(1)}, bf16[4,128,128]{2,1,0:T(8,128)(2,1)S(1)}, u32[]{:S(2)}, u32[]{:S(2)}) collective-permute-start(bf16[4,128,128]{2,1,0:T(8,128)(2,1)S(1)} %shard_map.94), channel_id=1, source_target_pairs={{0,4},{4,0},{8,12},{12,8},{16,20},{20,16},{24,28},{28,24},{1,5},{5... | collective-permute-start | bytes 393224 | tf_op jit(solution)/shard_map/ppermute | solution.py:32
  40.6 6.1 %collective-permute-start.18 = (bf16[1,128,128]{2,1,0:T(8,128)(2,1)S(1)}, bf16[1,128,128]{2,1,0:T(8,128)(2,1)S(1)}, u32[]{:S(2)}, u32[]{:S(2)}) collective-permute-start(bf16[1,128,128]{2,1,0:T(8,128)(2,1)S(1)} %get-tuple-element.77), channel_id=1, source_target_pairs={{0,16},{4,20},{8,24},{12,28},{16,0},{20,4},{24,8},{28,12},{1,17},{... | collective-permute-start | bytes 98312 | tf_op jit(solution)/shard_map/ppermute | solution.py:32
  43.2 5.5 %collective-permute-start.15 = (bf16[1,128,128]{2,1,0:T(8,128)(2,1)S(1)}, bf16[1,128,128]{2,1,0:T(8,128)(2,1)S(1)}, u32[]{:S(2)}, u32[]{:S(2)}) collective-permute-start(bf16[1,128,128]{2,1,0:T(8,128)(2,1)S(1)} %get-tuple-element.73.refs_0_), channel_id=1, source_target_pairs={{0,4},{4,0},{8,12},{12,8},{16,20},{20,16},{24,28},{28,24},{1,5},{5... | collective-permute-start | bytes 98312 | tf_op jit(solution)/shard_map/ppermute | solution.py:32
  43.7 6.5 %collective-permute-start.17 = (bf16[1,128,128]{2,1,0:T(8,128)(2,1)S(1)}, bf16[1,128,128]{2,1,0:T(8,128)(2,1)S(1)}, u32[]{:S(2)}, u32[]{:S(2)}) collective-permute-start(bf16[1,128,128]{2,1,0:T(8,128)(2,1)S(1)} %get-tuple-element.74), channel_id=1, source_target_pairs={{0,12},{4,8},{8,4},{12,0},{16,28},{20,24},{24,20},{28,16},{1,13},{... | collective-permute-start | bytes 98312 | tf_op jit(solution)/shard_map/ppermute | solution.py:32
  46.2 4.0 %collective-permute-start.16 = (bf16[1,128,128]{2,1,0:T(8,128)(2,1)S(1)}, bf16[1,128,128]{2,1,0:T(8,128)(2,1)S(1)}, u32[]{:S(2)}, u32[]{:S(2)}) collective-permute-start(bf16[1,128,128]{2,1,0:T(8,128)(2,1)S(1)} %get-tuple-element.74), channel_id=1, source_target_pairs={{0,8},{4,12},{8,0},{12,4},{16,24},{20,28},{24,16},{28,20},{1,9},{5... | collective-permute-start | bytes 98312 | tf_op jit(solution)/shard_map/ppermute | solution.py:32
  46.7 6.0 %collective-permute-start.21 = (bf16[1,128,128]{2,1,0:T(8,128)(2,1)S(1)}, bf16[1,128,128]{2,1,0:T(8,128)(2,1)S(1)}, u32[]{:S(2)}, u32[]{:S(2)}) collective-permute-start(bf16[1,128,128]{2,1,0:T(8,128)(2,1)S(1)} %shard_map.97.refs_0_), channel_id=1, source_target_pairs={{0,12},{4,8},{8,4},{12,0},{16,28},{20,24},{24,20},{28,16},{1,13},{... | collective-permute-start | bytes 98312 | tf_op jit(solution)/shard_map/ppermute | solution.py:32
  48.3 4.5 %collective-permute-start.20 = (bf16[1,128,128]{2,1,0:T(8,128)(2,1)S(1)}, bf16[1,128,128]{2,1,0:T(8,128)(2,1)S(1)}, u32[]{:S(2)}, u32[]{:S(2)}) collective-permute-start(bf16[1,128,128]{2,1,0:T(8,128)(2,1)S(1)} %shard_map.97.refs_0_), channel_id=1, source_target_pairs={{0,8},{4,12},{8,0},{12,4},{16,24},{20,28},{24,16},{28,20},{1,9},{5... | collective-permute-start | bytes 98312 | tf_op jit(solution)/shard_map/ppermute | solution.py:32
  48.7 4.1 %collective-permute-start.19 = (bf16[1,128,128]{2,1,0:T(8,128)(2,1)S(1)}, bf16[1,128,128]{2,1,0:T(8,128)(2,1)S(1)}, u32[]{:S(2)}, u32[]{:S(2)}) collective-permute-start(bf16[1,128,128]{2,1,0:T(8,128)(2,1)S(1)} %shard_map.97.refs_0_), channel_id=1, source_target_pairs={{0,4},{4,0},{8,12},{12,8},{16,20},{20,16},{24,28},{28,24},{1,5},{5... | collective-permute-start | bytes 98312 | tf_op jit(solution)/shard_map/ppermute | solution.py:32

commit v3 on v2

--- a/solution.py
+++ b/solution.py
@@ -88,7 +88,7 @@
     del value_ref, refs
 
 
-def tie(value, *after):
+def tie(value, *after, flops=0):
     return pl.pallas_call(
         tie_kernel,
         out_shape=pltpu.VMEM(value.shape, value.dtype),
@@ -96,6 +96,7 @@
         out_specs=VMEM,
         input_output_aliases={0: 0},
         compiler_params=pltpu.CompilerParams(vmem_limit_bytes=MIB),
+        cost_estimate=pl.CostEstimate(flops=flops, bytes_accessed=0, transcendentals=0),
     )(value, *after)
 
 
@@ -139,8 +140,8 @@
 
 def last_kernel(keys, span, heads, w_ref, g_ref, part_ref, *refs):
     segments, refs = refs[: len(keys)], refs[len(keys) :]
-    earlier, refs = refs[: -6 - (GROUP - 1)], refs[-6 - (GROUP - 1) :]
-    q_ref, k_ref, v_ref, state_ref, total_ref, near_ref, *sends = refs
+    earlier, refs = refs[: -5 - (GROUP - 1)], refs[-5 - (GROUP - 1) :]
+    q_ref, k_ref, v_ref, state_ref, total_ref, *sends = refs
     for j, out_ref in enumerate((q_ref, k_ref, v_ref)):
         term = project(w_ref, read_segments(segments, keys, span), j)
         out_ref[...] = (part_ref[j] + term).astype(BF16)
@@ -160,9 +161,6 @@
         for s in range(2):
             for e in range(share):
                 send[s, e] = total_ref[s, (place ^ m) * share + e].astype(BF16)
-    odd = bit_of(lax.axis_index("seq"), 0)
-    for h in range(heads):
-        near_ref[h] = jnp.where(odd, total_ref[1, h], total_ref[0, h]).astype(BF16)
 
 
 def local_kernel(span, heads, weight_ref, q_ref, k_ref, v_ref, g_ref, after_ref, out_ref):
@@ -194,23 +192,27 @@
 
 
 def owner_kernel(final, total_ref, *refs):
-    got, (near_ref, far_ref, sum_ref, next_ref) = refs[: GROUP - 1], refs[-4:]
+    got, refs = refs[: GROUP - 1], refs[GROUP - 1 :]
+    near_ref, far_ref, *nexts = refs[-3 if final else -4 :]
     position = lax.axis_index("seq")
     place = lax.rem(position, GROUP)
-    share = total_ref.shape[1] // GROUP
-    high = bit_of(position, 1)
+    heads = total_ref.shape[1]
+    share = heads // GROUP
+    odd, high = bit_of(position, 0), bit_of(position, 1)
     for e in range(share):
         mine, other = [], []
         for s in range(2):
             mine.append(total_ref[s, place * share + e] + got[0][s, e].astype(F32))
             other.append(got[1][s, e].astype(F32) + got[2][s, e].astype(F32))
+        sums = [mine[s] + other[s] for s in range(2)]
+        write_next(sums, e, 2, final, *nexts)
         near_ref[e] = jnp.where(high, other[0], other[1]).astype(BF16)
         far_ref[e] = jnp.where(high, mine[1], mine[0]).astype(BF16)
-        sums = [mine[s] + other[s] for s in range(2)]
-        write_next(sums, e, 2, final, sum_ref, next_ref)
-
-
-def write_next(sums, e, bit, final, sum_ref, next_ref):
+    for h in range(heads):
+        near_ref[share + h] = jnp.where(odd, total_ref[1, h], total_ref[0, h]).astype(BF16)
+
+
+def write_next(sums, e, bit, final, next_ref, sum_ref=None):
     if final:
         value = jnp.where(bit_of(lax.axis_index("seq"), bit), sums[1], sums[0])
         next_ref[e] = value.astype(BF16)
@@ -220,13 +222,13 @@
         next_ref[s, e] = sums[s].astype(BF16)
 
 
-def climb_kernel(bit, next_final, got_ref, old_ref, level_ref, sum_ref, next_ref):
+def climb_kernel(bit, next_final, got_ref, old_ref, level_ref, *nexts):
     on = bit_of(lax.axis_index("seq"), bit)
     for e in range(got_ref.shape[1]):
         both = [got_ref[s, e].astype(F32) for s in range(2)]
         level_ref[e] = jnp.where(on, both[0], both[1]).astype(BF16)
         sums = [old_ref[s, e] + both[s] for s in range(2)]
-        write_next(sums, e, bit + 1, next_final, sum_ref, next_ref)
+        write_next(sums, e, bit + 1, next_final, *nexts)
 
 
 def pair_block(first, second):
@@ -279,7 +281,7 @@
         copy.wait()
 
 
-def early_side_kernel(spans, heads, top, weight_ref, g_ref, near_ref, *refs):
+def early_side_kernel(spans, heads, top, weight_ref, g_ref, *refs):
     chunks = len(spans)
     levels, refs = refs[: (top - 1) * GROUP], refs[(top - 1) * GROUP :]
     q_refs, refs = refs[:chunks], refs[chunks:]
@@ -301,7 +303,7 @@
         found = []
         for h in range(heads):
             coef = jnp.where(taken, weight_ref[h, 1] * norm, 0.0)
-            found.append(mix_ref[h] + coef * near_ref[h].astype(F32))
+            found.append(mix_ref[h] + coef * levels[1][heads // GROUP + h].astype(F32))
         return found
 
     def add(sums, side, c):
@@ -356,17 +358,16 @@
             )
 
 
-def exchange(totals, near, sends, local, late):
+def exchange(totals, sends, local, late):
     depth = lax.axis_size("seq").bit_length() - 1
     heads, square = totals.shape[1], totals.shape[2:]
     share = heads // GROUP
     last = depth - 1
 
-    def message(bit):
-        return pltpu.VMEM((share, *square) if bit == last else (2, share, *square), BF16)
-
-    def running(bit):
-        return pltpu.VMEM((1, 8, 128) if bit == last else (2, share, *square), F32)
+    def nexts(bit):
+        if bit == last:
+            return [pltpu.VMEM((share, *square), BF16)]
+        return [pltpu.VMEM((2, share, *square), BF16), pltpu.VMEM((2, share, *square), F32)]
 
     def spread(mine, other):
         return [mine, *[swap(mine if m == 1 else other, "seq", m) for m in range(1, GROUP)]]
@@ -374,27 +375,26 @@
     one = pltpu.VMEM((share, *square), BF16)
     got = [swap(send, "seq", m) for m, send in enumerate(sends, 1)]
     fillers = [local(c, sends[0]) for c in late]
-    near = swap(tie(near, *fillers), "seq", 1)
-    mine, other, sums, sent = call(
+    mine, other, sent, *sums = call(
         functools.partial(owner_kernel, last == 2),
-        [one, one, running(2), message(2)],
+        [pltpu.VMEM((share + heads, *square), BF16), one, *nexts(2)],
         [totals, *got, *fillers],
         [VMEM] * GROUP + [ANY] * len(fillers),
-        5 * 10**9,
+        10**6,
     )
     levels = spread(mine, other)
     for bit in range(2, last):
-        found, sums, sent = call(
+        found, sent, *sums = call(
             functools.partial(climb_kernel, bit, bit + 1 == last),
-            [one, running(bit + 1), message(bit + 1)],
-            [swap(sent, "seq", 1 << bit), sums],
+            [one, *nexts(bit + 1)],
+            [swap(sent, "seq", 1 << bit), *sums],
             [VMEM] * 2,
             10**6,
         )
         levels += spread(found, found)
-    found = tie(swap(sent, "seq", 1 << last), near)
+    found = tie(swap(sent, "seq", 1 << last), mine, flops=12 * 10**8)
     levels += spread(found, found)
-    return near, levels, fillers
+    return levels, fillers
 
 
 def per_device(inputs, w_qkv, level_weight, grad_out):
@@ -468,7 +468,6 @@
                     flat,
                     state,
                     state,
-                    pltpu.VMEM((heads, size, size), BF16),
                     *[pltpu.VMEM((2, heads // GROUP, size, size), BF16)] * (GROUP - 1),
                 ],
                 operands,
@@ -480,7 +479,7 @@
         vs.append(got[2])
         states.append(got[3])
         after = got[3]
-    near, levels, fillers = exchange(got[4], got[5], got[6:], local, range(len(locals_), CHUNKS))
+    levels, fillers = exchange(got[4], got[5:], local, range(len(locals_), CHUNKS))
     locals_ += fillers
     shapes = [jax.ShapeDtypeStruct((rows, width), BF16)] * 4
     top = len(levels) // GROUP
@@ -490,7 +489,7 @@
         pltpu.VMEM((heads, size, size), F32),
         pltpu.SemaphoreType.DMA((2, CHUNKS)),
     ]
-    operands = [level_weight, grads, near, *levels[:-GROUP], *flats, *states, *locals_]
+    operands = [level_weight, grads, *levels[:-GROUP], *flats, *states, *locals_]
     *written, base = call(
         functools.partial(early_side_kernel, spans, heads, top),
         [*shapes, pltpu.VMEM((CHUNKS, heads, size, size), F32)],

time: 55.5 us -> 54.3 us (0.978)
  starting transfers between devices: 23.6 us -> 21.9 us
  waiting for transfers between devices: 2.14 us -> 3.29 us
  Pallas kernels: 28.5 us -> 27.9 us
    ppermute x22 -> x21, starting transfers between devices: 23.6 us -> 21.9 us  [swap(): return lax.ppermute(value, axis, pairs)]
    ppermute x22 -> x21, waiting for transfers between devices: 2.14 us -> 3.29 us  [swap(): return lax.ppermute(value, axis, pairs)]
    pallas_call x17, Pallas kernels: 28.5 us -> 27.9 us  [call(): pl.pallas_call(kernel, out_shape=outs, in_specs=specs, out_specs=[VMEM] *...]
  transfers between devices with their start and end apart: 22 -> 21, of which waited for: 4 -> 6; matrix products, arithmetic and copies ran while one was open for 0% -> 0% of each run, Pallas kernels for 46% -> 45%
where the time goes in v3:
time: 54.3 us; the launch traced here: 54.2 us
  Pallas kernels  27.9 us (51%)
  starting transfers between devices  21.9 us (40%)
  waiting for transfers between devices  3.29 us (6%)
  between operations  1.01 us (2%)
    pallas_call x17, Pallas kernels, call(): pl.pallas_call(kernel, out_shape=outs, in_specs=specs, out_specs=[VMEM] *...  27.9 us
    ppermute x21, starting transfers between devices, swap(): return lax.ppermute(value, axis, pairs)  21.9 us
    ppermute x21, waiting for transfers between devices, swap(): return lax.ppermute(value, axis, pairs)  3.29 us
  transfers between devices with their start and end apart: 21, of which 6 were waited for; matrix products, arithmetic and copies ran while one was open for 0% of the time, Pallas kernels for 45%

profile of v3, /device:TPU:0, one launch (start us, length us, event | category | flops | bytes accessed | tf_op | source)
XLA Modules:
  0.0 54.2 jit_solution(7713413298955333857)
XLA Ops:
  0.6 0.5 collective-permute-start
  1.1 0.9 %shard_map.75.refs_1_.refs_0_ = bf16[160,512]{1,0:T(8,128)(2,1)S(1)} custom-call(bf16[1024,512]{1,0:T(8,128)(2,1)} %refs_0_.4), custom_call_target="tpu_custom_call" | custom-call | bytes 327680 | tf_op jit(solution)/shard_map/pallas_call | solution.py:40
  2.1 2.6 %collective-permute-start.5 = (bf16[160,512]{1,0:T(8,128)(2,1)S(1)}, bf16[160,512]{1,0:T(8,128)(2,1)S(1)}, u32[]{:S(2)}, u32[]{:S(2)}) collective-permute-start(bf16[160,512]{1,0:T(8,128)(2,1)S(1)} %shard_map.75.refs_1_.refs_0_), channel_id=1, source_target_pairs={{0,2},{1,3},{2,0},{3,1},{4,6},{5,7},{6,4},{7,5},{8,10},{9,11},{10,... | collective-permute-start | bytes 491528 | tf_op jit(solution)/shard_map/ppermute | solution.py:32
  4.7 1.3 %shard_map.76 = (bf16[192,512]{1,0:T(8,128)(2,1)S(1)}, bf16[208,512]{1,0:T(8,128)(2,1)S(1)}, bf16[224,512]{1,0:T(8,128)(2,1)S(1)}, bf16[240,512]{1,0:T(8,128)(2,1)S(1)}) custom-call(bf16[1024,512]{1,0:T(8,128)(2,1)} %refs_0_.4, bf16[160,512]{1,0:T(8,128)(2,1)S(1)} %shard_map.75.refs_1_.refs_0_), custom_call_target="tpu_custom_call" | custom-call | bytes 1769472 | tf_op jit(solution)/shard_map/pallas_call | solution.py:40
  6.0 0.1 collective-permute-start.4
  6.1 3.1 %shard_map.77 = (bf16[1024,512]{1,0:T(8,128)(2,1)S(1)}, bf16[3,2048,512]{2,1,0:T(8,128)(2,1)S(1)}) custom-call(bf16[1024,512]{1,0:T(8,128)(2,1)} %refs_0_.5, bf16[3,2048,512]{2,1,0:T(8,128)(2,1)} %refs_1_.1, bf16[192,512]{1,0:T(8,128)(2,1)S(1)} %get-tuple-element.42.refs_2_.refs_0_), custom_call_target="tpu_custom_call" | custom-call | bytes 14680064 | tf_op jit(solution)/shard_map/pallas_call | solution.py:40
  9.2 0.5 collective-permute-done.5.value_ref
  9.7 1.9 %collective-permute-start.3 = (bf16[208,512]{1,0:T(8,128)(2,1)S(1)}, bf16[208,512]{1,0:T(8,128)(2,1)S(1)}, u32[]{:S(2)}, u32[]{:S(2)}) collective-permute-start(bf16[208,512]{1,0:T(8,128)(2,1)S(1)} %get-tuple-element.47.refs_0_), channel_id=1, source_target_pairs={{0,2},{1,3},{2,0},{3,1},{4,6},{5,7},{6,4},{7,5},{8,10},{9,11},{10,... | collective-permute-start | bytes 638984 | tf_op jit(solution)/shard_map/ppermute | solution.py:32
  11.7 0.0 collective-permute-done.6.refs_3_
  11.7 0.0 collective-permute-done.refs_1_
  11.7 1.5 %shard_map.79 = (bf16[160,512]{1,0:T(8,128)(2,1)S(1)}, bf16[160,512]{1,0:T(8,128)(2,1)S(1)}, bf16[160,512]{1,0:T(8,128)(2,1)S(1)}, f32[2,4,128,128]{3,2,1,0:T(8,128)S(1)}) custom-call(bf16[3,2048,512]{2,1,0:T(8,128)(2,1)S(1)} %get-tuple-element.44.refs_0_.w_ref, bf16[1024,512]{1,0:T(8,128)(2,1)S(1)} %get-tuple-element.43.g_ref, ...), custom_call_target="tpu_custom_call" | custom-call | tf_op jit(solution)/shard_map/pallas_call | solution.py:40
  13.2 0.7 %collective-permute-done.4.value_ref = bf16[192,512]{1,0:T(8,128)(2,1)S(1)} collective-permute-done((bf16[192,512]{1,0:T(8,128)(2,1)S(1)}, bf16[192,512]{1,0:T(8,128)(2,1)S(1)}, u32[]{:S(2)}, u32[]{:S(2)}) %collective-permute-start.4) | collective-permute-done | bytes 196640 | tf_op jit(solution)/shard_map/ppermute | solution.py:32
  13.9 0.0 collective-permute-start.7
  13.9 1.9 %collective-permute-start.2 = (bf16[224,512]{1,0:T(8,128)(2,1)S(1)}, bf16[224,512]{1,0:T(8,128)(2,1)S(1)}, u32[]{:S(2)}, u32[]{:S(2)}) collective-permute-start(bf16[224,512]{1,0:T(8,128)(2,1)S(1)} %get-tuple-element.46.refs_0_), channel_id=1, source_target_pairs={{0,2},{1,3},{2,0},{3,1},{4,6},{5,7},{6,4},{7,5},{8,10},{9,11},{10,... | collective-permute-start | bytes 688136 | tf_op jit(solution)/shard_map/ppermute | solution.py:32
  15.9 1.4 %shard_map.81.refs_4_.refs_24_.refs_19_ = f32[4,160,512]{2,1,0:T(8,128)S(1)} custom-call(f32[4,4]{1,0:T(4,128)S(1)} %copy-done, bf16[160,512]{1,0:T(8,128)(2,1)S(1)} %get-tuple-element.49.q_ref.refs_4_, bf16[160,512]{1,0:T(8,128)(2,1)S(1)} %get-tuple-element.50.k_ref.refs_9_, bf16[160,512]{1,0:T(8,128)(2,1)S(1)} %get-tuple-element.51.v_ref.refs_14_, ...), custom_call_target="tpu_custom_call" | custom-call | tf_op jit(solution)/shard_map/pallas_call | solution.py:40
  17.3 1.7 %shard_map.82 = (bf16[192,512]{1,0:T(8,128)(2,1)S(1)}, bf16[192,512]{1,0:T(8,128)(2,1)S(1)}, bf16[192,512]{1,0:T(8,128)(2,1)S(1)}, f32[2,4,128,128]{3,2,1,0:T(8,128)S(1)}) custom-call(bf16[3,2048,512]{2,1,0:T(8,128)(2,1)S(1)} %get-tuple-element.44.refs_0_.w_ref, bf16[1024,512]{1,0:T(8,128)(2,1)S(1)} %get-tuple-element.43.g_ref, ...), custom_call_target="tpu_custom_call" | custom-call | tf_op jit(solution)/shard_map/pallas_call | solution.py:40
  19.1 0.0 collective-permute-done.3.value_ref
  19.1 0.3 collective-permute-start.8
  19.4 1.1 %collective-permute-start.1 = (bf16[240,512]{1,0:T(8,128)(2,1)S(1)}, bf16[240,512]{1,0:T(8,128)(2,1)S(1)}, u32[]{:S(2)}, u32[]{:S(2)}) collective-permute-start(bf16[240,512]{1,0:T(8,128)(2,1)S(1)} %get-tuple-element.45.refs_0_), channel_id=1, source_target_pairs={{0,2},{1,3},{2,0},{3,1},{4,6},{5,7},{6,4},{7,5},{8,10},{9,11},{10,... | collective-permute-start | bytes 737288 | tf_op jit(solution)/shard_map/ppermute | solution.py:32
  20.5 1.6 %shard_map.84.refs_4_.refs_25_.refs_20_ = f32[4,192,512]{2,1,0:T(8,128)S(1)} custom-call(f32[4,4]{1,0:T(4,128)S(1)} %copy-done, bf16[192,512]{1,0:T(8,128)(2,1)S(1)} %get-tuple-element.53.q_ref.refs_5_, bf16[192,512]{1,0:T(8,128)(2,1)S(1)} %get-tuple-element.54.k_ref.refs_10_, bf16[192,512]{1,0:T(8,128)(2,1)S(1)} %get-tuple-element.55.v_ref.refs_15_, ...), custom_call_target="tpu_custom_call" | custom-call | tf_op jit(solution)/shard_map/pallas_call | solution.py:40
  22.0 1.8 %shard_map.85 = (bf16[208,512]{1,0:T(8,128)(2,1)S(1)}, bf16[208,512]{1,0:T(8,128)(2,1)S(1)}, bf16[208,512]{1,0:T(8,128)(2,1)S(1)}, f32[2,4,128,128]{3,2,1,0:T(8,128)S(1)}) custom-call(bf16[3,2048,512]{2,1,0:T(8,128)(2,1)S(1)} %get-tuple-element.44.refs_0_.w_ref, bf16[1024,512]{1,0:T(8,128)(2,1)S(1)} %get-tuple-element.43.g_ref, ...), custom_call_target="tpu_custom_call" | custom-call | tf_op jit(solution)/shard_map/pallas_call | solution.py:40
  23.9 0.3 collective-permute-start.9
  24.2 1.6 %shard_map.87.refs_4_.refs_26_.refs_21_ = f32[4,208,512]{2,1,0:T(8,128)S(1)} custom-call(f32[4,4]{1,0:T(4,128)S(1)} %copy-done, bf16[208,512]{1,0:T(8,128)(2,1)S(1)} %get-tuple-element.57.q_ref.refs_6_, bf16[208,512]{1,0:T(8,128)(2,1)S(1)} %get-tuple-element.58.k_ref.refs_11_, bf16[208,512]{1,0:T(8,128)(2,1)S(1)} %get-tuple-element.59.v_ref.refs_16_, ...), custom_call_target="tpu_custom_call" | custom-call | tf_op jit(solution)/shard_map/pallas_call | solution.py:40
  25.9 1.9 %shard_map.88 = (bf16[224,512]{1,0:T(8,128)(2,1)S(1)}, bf16[224,512]{1,0:T(8,128)(2,1)S(1)}, bf16[224,512]{1,0:T(8,128)(2,1)S(1)}, f32[2,4,128,128]{3,2,1,0:T(8,128)S(1)}) custom-call(bf16[3,2048,512]{2,1,0:T(8,128)(2,1)S(1)} %get-tuple-element.44.refs_0_.w_ref, bf16[1024,512]{1,0:T(8,128)(2,1)S(1)} %get-tuple-element.43.g_ref, ...), custom_call_target="tpu_custom_call" | custom-call | tf_op jit(solution)/shard_map/pallas_call | solution.py:40
  27.8 0.7 %collective-permute-done.1.value_ref = bf16[240,512]{1,0:T(8,128)(2,1)S(1)} collective-permute-done((bf16[240,512]{1,0:T(8,128)(2,1)S(1)}, bf16[240,512]{1,0:T(8,128)(2,1)S(1)}, u32[]{:S(2)}, u32[]{:S(2)}) %collective-permute-start.1) | collective-permute-done | bytes 245792 | tf_op jit(solution)/shard_map/ppermute | solution.py:32
  28.5 1.3 %shard_map.90.part_ref = f32[3,240,512]{2,1,0:T(8,128)S(1)} custom-call(bf16[3,2048,512]{2,1,0:T(8,128)(2,1)S(1)} %get-tuple-element.44.refs_0_.w_ref, bf16[240,512]{1,0:T(8,128)(2,1)S(1)} %get-tuple-element.45.refs_0_, bf16[1024,512]{1,0:T(8,128)(2,1)S(1)} %collective-permute-done.refs_1_, bf16[240,512]{1,0:T(8,128)(2,1)S(1)} %shard_map.89.refs_2_), custom_call_target="tpu_custom_call" | custom-call | tf_op jit(solution)/shard_map/pallas_call | solution.py:40
  29.8 0.2 collective-permute-done.10.refs_0_
  30.0 0.9 %shard_map.91 = (bf16[240,512]{1,0:T(8,128)(2,1)S(1)}, bf16[240,512]{1,0:T(8,128)(2,1)S(1)}, bf16[240,512]{1,0:T(8,128)(2,1)S(1)}, f32[2,4,128,128]{3,2,1,0:T(8,...) custom-call(bf16[3,2048,512]{2,1,0:T(8,128)(2,1)S(1)} %get-tuple-ele, ...), custom_call_target="tpu_custom_call" | custom-call | tf_op jit(solution)/shard_map/pallas_call | solution.py:40
  30.9 1.9 %collective-permute-start.12 = (bf16[2,1,128,128]{3,2,1,0:T(8,128)(2,1)S(1)}, bf16[2,1,128,128]{3,2,1,0:T(8,128)(2,1)S(1)}, u32[]{:S(2)}, u32[]{:S(2)}) collective-permute-start(bf16[2,1,128,128]{3,2,1,0:T(8,128)(2,1)S(1)} %get-tuple-element.63), channel_id=1, source_target_pairs={{0,8},{4,12},{8,0},{12,4},{16,24},{20,28},{24,16},{28,20},{1,9},{5... | collective-permute-start | bytes 196616 | tf_op jit(solution)/shard_map/ppermute | solution.py:32
  32.8 1.4 %collective-permute-start.13 = (bf16[2,1,128,128]{3,2,1,0:T(8,128)(2,1)S(1)}, bf16[2,1,128,128]{3,2,1,0:T(8,128)(2,1)S(1)}, u32[]{:S(2)}, u32[]{:S(2)}) collective-permute-start(bf16[2,1,128,128]{3,2,1,0:T(8,128)(2,1)S(1)} %get-tuple-element.64), channel_id=1, source_target_pairs={{0,12},{4,8},{8,4},{12,0},{16,28},{20,24},{24,20},{28,16},{1,13},{... | collective-permute-start | bytes 196616 | tf_op jit(solution)/shard_map/ppermute | solution.py:32
  34.2 0.3 collective-permute-start.11
  34.5 1.8 %shard_map.93.refs_4_.refs_28_.refs_23_ = f32[4,240,512]{2,1,0:T(8,128)S(1)} custom-call(f32[4,4]{1,0:T(4,128)S(1)} %copy-done, bf16[240,512]{1,0:T(8,128)(2,1)S(1)} %get-tuple-element.68.q_ref.refs_8_, bf16[240,512]{1,0:T(8,128)(2,1)S(1)} %get-tuple-element.69.k_ref.refs_13_, bf16[240,512]{1,0:T(8,128)(2,1)S(1)} %get-tuple-element.70.v_ref.refs_18_, ...), custom_call_target="tpu_custom_call" | custom-call | flops 2949120000 | tf_op jit(solution)/shard_map/pallas_call | solution.py:40
  36.3 1.9 %shard_map.92.refs_3_.refs_27_.refs_22_ = f32[4,224,512]{2,1,0:T(8,128)S(1)} custom-call(f32[4,4]{1,0:T(4,128)S(1)} %copy-done, bf16[224,512]{1,0:T(8,128)(2,1)S(1)} %get-tuple-element.65.q_ref.refs_7_, bf16[224,512]{1,0:T(8,128)(2,1)S(1)} %get-tuple-element.66.k_ref.refs_12_, bf16[224,512]{1,0:T(8,128)(2,1)S(1)} %get-tuple-element.67.v_ref.refs_17_, ...), custom_call_target="tpu_custom_call" | custom-call | flops 2569011200 | tf_op jit(solution)/shard_map/pallas_call | solution.py:40
  38.2 0.0 collective-permute-done.13.refs_2_
  38.2 1.0 %collective-permute-done.11.refs_0_ = bf16[2,1,128,128]{3,2,1,0:T(8,128)(2,1)S(1)} collective-permute-done((bf16[2,1,128,128]{3,2,1,0:T(8,128)(2,1)S(1)}, bf16[2,1,128,128]{3,2,1,0:T(8,128)(2,1)S(1)}, u32[]{:S(2)}, u32[]{:S(2)}) %collective-permute-start.11) | collective-permute-done | bytes 65568 | tf_op jit(solution)/shard_map/ppermute | solution.py:32
  39.2 0.1 shard_map.94
  39.3 2.7 %collective-permute-start.17 = (bf16[1,128,128]{2,1,0:T(8,128)(2,1)S(1)}, bf16[1,128,128]{2,1,0:T(8,128)(2,1)S(1)}, u32[]{:S(2)}, u32[]{:S(2)}) collective-permute-start(bf16[1,128,128]{2,1,0:T(8,128)(2,1)S(1)} %get-tuple-element.75), channel_id=1, source_target_pairs={{0,16},{4,20},{8,24},{12,28},{16,0},{20,4},{24,8},{28,12},{1,17},{... | collective-permute-start | bytes 98312 | tf_op jit(solution)/shard_map/ppermute | solution.py:32
  41.9 0.7 %collective-permute-start.14 = (bf16[5,128,128]{2,1,0:T(8,128)(2,1)S(1)}, bf16[5,128,128]{2,1,0:T(8,128)(2,1)S(1)}, u32[]{:S(2)}, u32[]{:S(2)}) collective-permute-start(bf16[5,128,128]{2,1,0:T(8,128)(2,1)S(1)} %get-tuple-element.71.refs_0_), channel_id=1, source_target_pairs={{0,4},{4,0},{8,12},{12,8},{16,20},{20,16},{24,28},{28,24},{1,5},{5... | collective-permute-start | bytes 491528 | tf_op jit(solution)/shard_map/ppermute | solution.py:32
  42.7 2.1 %collective-permute-start.16 = (bf16[1,128,128]{2,1,0:T(8,128)(2,1)S(1)}, bf16[1,128,128]{2,1,0:T(8,128)(2,1)S(1)}, u32[]{:S(2)}, u32[]{:S(2)}) collective-permute-start(bf16[1,128,128]{2,1,0:T(8,128)(2,1)S(1)} %get-tuple-element.72), channel_id=1, source_target_pairs={{0,12},{4,8},{8,4},{12,0},{16,28},{20,24},{24,20},{28,16},{1,13},{... | collective-permute-start | bytes 98312 | tf_op jit(solution)/shard_map/ppermute | solution.py:32
  44.8 0.6 %collective-permute-start.15 = (bf16[1,128,128]{2,1,0:T(8,128)(2,1)S(1)}, bf16[1,128,128]{2,1,0:T(8,128)(2,1)S(1)}, u32[]{:S(2)}, u32[]{:S(2)}) collective-permute-start(bf16[1,128,128]{2,1,0:T(8,128)(2,1)S(1)} %get-tuple-element.72), channel_id=1, source_target_pairs={{0,8},{4,12},{8,0},{12,4},{16,24},{20,28},{24,16},{28,20},{1,9},{5... | collective-permute-start | bytes 98312 | tf_op jit(solution)/shard_map/ppermute | solution.py:32
  45.4 0.0 collective-permute-done.17.value_ref
  45.4 1.8 %collective-permute-start.20 = (bf16[1,128,128]{2,1,0:T(8,128)(2,1)S(1)}, bf16[1,128,128]{2,1,0:T(8,128)(2,1)S(1)}, u32[]{:S(2)}, u32[]{:S(2)}) collective-permute-start(bf16[1,128,128]{2,1,0:T(8,128)(2,1)S(1)} %shard_map.96.refs_0_), channel_id=1, source_target_pairs={{0,12},{4,8},{8,4},{12,0},{16,28},{20,24},{24,20},{28,16},{1,13},{... | collective-permute-start | bytes 98312 | tf_op jit(solution)/shard_map/ppermute | solution.py:32
  47.2 0.4 collective-permute-start.19
  47.6 0.0 collective-permute-done.16.refs_3_
  47.6 1.3 %collective-permute-start.18 = (bf16[1,128,128]{2,1,0:T(8,128)(2,1)S(1)}, bf16[1,128,128]{2,1,0:T(8,128)(2,1)S(1)}, u32[]{:S(2)}, u32[]{:S(2)}) collective-permute-start(bf16[1,128,128]{2,1,0:T(8,128)(2,1)S(1)} %shard_map.96.refs_0_), channel_id=1, source_target_pairs={{0,4},{4,0},{8,12},{12,8},{16,20},{20,16},{24,28},{28,24},{1,5},{5... | collective-permute-start | bytes 98312 | tf_op jit(solution)/shard_map/ppermute | solution.py:32
  48.9 0.2 collective-permute-done.14.refs_1_
  49.1 2.5 %shard_map.95 = (bf16[1024,512]{1,0:T(8,128)(2,1)}, bf16[1024,512]{1,0:T(8,128)(2,1)}, bf16[1024,512]{1,0:T(8,128)(2,1)}, bf16[1024,512]{1,0:T(8,128)(2,1)}, f32[5,4,128,128]{3,2,1,0:T(8,128)S(1)}) custom-call(f32[4,4]{1,0:T(4,128)S(1)} %copy-done, bf16[1024,512]{1,0:T(8,128)(2,1)S(1)} %get-tuple-element.43.g_ref, ...), custom_call_target="tpu_custom_call" | custom-call | tf_op jit(solution)/shard_map/pallas_call | solution.py:40
  51.6 2.4 %shard_map.97 = (bf16[1024,512]{1,0:T(8,128)(2,1)}, bf16[1024,512]{1,0:T(8,128)(2,1)}, bf16[1024,512]{1,0:T(8,128)(2,1)}, bf16[1024,512]{1,0:T(8,128)(2,1)}) custom-call(f32[4,4]{1,0:T(4,128)S(1)} %copy-done, bf16[1024,512]{1,0:T(8,128)(2,1)S(1)} %get-tuple-element.43.g_ref, ...), custom_call_target="tpu_custom_call", output_to_operand_aliasing={{0}: (27, {}), {1}: (28, {}), {2}: (29, {}), {3}: (30, {})} | custom-call | tf_op jit(solution)/shard_map/pallas_call | solution.py:40
  (19 shorter events, 0.0 us)
Async XLA Ops:
  0.6 11.1 %collective-permute-start = (bf16[1024,512]{1,0:T(8,128)(2,1)}, bf16[1024,512]{1,0:T(8,128)(2,1)S(1)}, u32[]{:S(2)}, u32[]{:S(2)}) collective-permute-start(bf16[1024,512]{1,0:T(8,128)(2,1)} %refs_0_.4), channel_id=1, source_target_pairs={{0,1},{1,0},{2,3},{3,2},{4,5},{5,4},{6,7},{7,6},{8,9},{9,8},{10,11... | collective-permute-start | bytes 3145736 | tf_op jit(solution)/shard_map/ppermute | solution.py:32
  2.1 7.6 %collective-permute-start.5 = (bf16[160,512]{1,0:T(8,128)(2,1)S(1)}, bf16[160,512]{1,0:T(8,128)(2,1)S(1)}, u32[]{:S(2)}, u32[]{:S(2)}) collective-permute-start(bf16[160,512]{1,0:T(8,128)(2,1)S(1)} %shard_map.75.refs_1_.refs_0_), channel_id=1, source_target_pairs={{0,2},{1,3},{2,0},{3,1},{4,6},{5,7},{6,4},{7,5},{8,10},{9,11},{10,... | collective-permute-start | bytes 491528 | tf_op jit(solution)/shard_map/ppermute | solution.py:32
  6.0 8.0 %collective-permute-start.4 = (bf16[192,512]{1,0:T(8,128)(2,1)S(1)}, bf16[192,512]{1,0:T(8,128)(2,1)S(1)}, u32[]{:S(2)}, u32[]{:S(2)}) collective-permute-start(bf16[192,512]{1,0:T(8,128)(2,1)S(1)} %get-tuple-element.42.refs_2_.refs_0_), channel_id=1, source_target_pairs={{0,2},{1,3},{2,0},{3,1},{4,6},{5,7},{6,4},{7,5},{8,10},{9,11},{10,... | collective-permute-start | bytes 589832 | tf_op jit(solution)/shard_map/ppermute | solution.py:32
  9.7 2.0 %collective-permute-start.6 = (bf16[160,512]{1,0:T(8,128)(2,1)S(1)}, bf16[160,512]{1,0:T(8,128)(2,1)S(1)}, u32[]{:S(2)}, u32[]{:S(2)}) collective-permute-start(bf16[160,512]{1,0:T(8,128)(2,1)S(1)} %shard_map.78.refs_2_), channel_id=1, source_target_pairs={{0,1},{1,0},{2,3},{3,2},{4,5},{5,4},{6,7},{7,6},{8,9},{9,8},{10,11... | collective-permute-start | bytes 491528 | tf_op jit(solution)/shard_map/ppermute | solution.py:32
  9.7 9.4 %collective-permute-start.3 = (bf16[208,512]{1,0:T(8,128)(2,1)S(1)}, bf16[208,512]{1,0:T(8,128)(2,1)S(1)}, u32[]{:S(2)}, u32[]{:S(2)}) collective-permute-start(bf16[208,512]{1,0:T(8,128)(2,1)S(1)} %get-tuple-element.47.refs_0_), channel_id=1, source_target_pairs={{0,2},{1,3},{2,0},{3,1},{4,6},{5,7},{6,4},{7,5},{8,10},{9,11},{10,... | collective-permute-start | bytes 638984 | tf_op jit(solution)/shard_map/ppermute | solution.py:32
  11.7 4.2 %copy-start = (f32[4,4]{1,0:T(4,128)S(1)}, f32[4,4]{1,0:T(4,128)}, u32[]{:S(2)}) copy-start(f32[4,4]{1,0:T(4,128)} %weight_ref.13) | copy-start | bytes 196
  13.9 3.4 %collective-permute-start.7 = (bf16[192,512]{1,0:T(8,128)(2,1)S(1)}, bf16[192,512]{1,0:T(8,128)(2,1)S(1)}, u32[]{:S(2)}, u32[]{:S(2)}) collective-permute-start(bf16[192,512]{1,0:T(8,128)(2,1)S(1)} %shard_map.80.after_ref.refs_2_), channel_id=1, source_target_pairs={{0,1},{1,0},{2,3},{3,2},{4,5},{5,4},{6,7},{7,6},{8,9},{9,8},{10,11... | collective-permute-start | bytes 589832 | tf_op jit(solution)/shard_map/ppermute | solution.py:32
  13.9 9.9 %collective-permute-start.2 = (bf16[224,512]{1,0:T(8,128)(2,1)S(1)}, bf16[224,512]{1,0:T(8,128)(2,1)S(1)}, u32[]{:S(2)}, u32[]{:S(2)}) collective-permute-start(bf16[224,512]{1,0:T(8,128)(2,1)S(1)} %get-tuple-element.46.refs_0_), channel_id=1, source_target_pairs={{0,2},{1,3},{2,0},{3,1},{4,6},{5,7},{6,4},{7,5},{8,10},{9,11},{10,... | collective-permute-start | bytes 688136 | tf_op jit(solution)/shard_map/ppermute | solution.py:32
  19.1 2.9 %collective-permute-start.8 = (bf16[208,512]{1,0:T(8,128)(2,1)S(1)}, bf16[208,512]{1,0:T(8,128)(2,1)S(1)}, u32[]{:S(2)}, u32[]{:S(2)}) collective-permute-start(bf16[208,512]{1,0:T(8,128)(2,1)S(1)} %shard_map.83.after_ref.refs_2_), channel_id=1, source_target_pairs={{0,1},{1,0},{2,3},{3,2},{4,5},{5,4},{6,7},{7,6},{8,9},{9,8},{10,11... | collective-permute-start | bytes 638984 | tf_op jit(solution)/shard_map/ppermute | solution.py:32
  19.4 9.1 %collective-permute-start.1 = (bf16[240,512]{1,0:T(8,128)(2,1)S(1)}, bf16[240,512]{1,0:T(8,128)(2,1)S(1)}, u32[]{:S(2)}, u32[]{:S(2)}) collective-permute-start(bf16[240,512]{1,0:T(8,128)(2,1)S(1)} %get-tuple-element.45.refs_0_), channel_id=1, source_target_pairs={{0,2},{1,3},{2,0},{3,1},{4,6},{5,7},{6,4},{7,5},{8,10},{9,11},{10,... | collective-permute-start | bytes 737288 | tf_op jit(solution)/shard_map/ppermute | solution.py:32
  23.9 1.9 %collective-permute-start.9 = (bf16[224,512]{1,0:T(8,128)(2,1)S(1)}, bf16[224,512]{1,0:T(8,128)(2,1)S(1)}, u32[]{:S(2)}, u32[]{:S(2)}) collective-permute-start(bf16[224,512]{1,0:T(8,128)(2,1)S(1)} %shard_map.86.after_ref.refs_2_), channel_id=1, source_target_pairs={{0,1},{1,0},{2,3},{3,2},{4,5},{5,4},{6,7},{7,6},{8,9},{9,8},{10,11... | collective-permute-start | bytes 688136 | tf_op jit(solution)/shard_map/ppermute | solution.py:32
  28.5 1.5 %collective-permute-start.10 = (bf16[240,512]{1,0:T(8,128)(2,1)S(1)}, bf16[240,512]{1,0:T(8,128)(2,1)S(1)}, u32[]{:S(2)}, u32[]{:S(2)}) collective-permute-start(bf16[240,512]{1,0:T(8,128)(2,1)S(1)} %shard_map.89.refs_2_), channel_id=1, source_target_pairs={{0,1},{1,0},{2,3},{3,2},{4,5},{5,4},{6,7},{7,6},{8,9},{9,8},{10,11... | collective-permute-start | bytes 737288 | tf_op jit(solution)/shard_map/ppermute | solution.py:32
  30.9 7.3 %collective-permute-start.12 = (bf16[2,1,128,128]{3,2,1,0:T(8,128)(2,1)S(1)}, bf16[2,1,128,128]{3,2,1,0:T(8,128)(2,1)S(1)}, u32[]{:S(2)}, u32[]{:S(2)}) collective-permute-start(bf16[2,1,128,128]{3,2,1,0:T(8,128)(2,1)S(1)} %get-tuple-element.63), channel_id=1, source_target_pairs={{0,8},{4,12},{8,0},{12,4},{16,24},{20,28},{24,16},{28,20},{1,9},{5... | collective-permute-start | bytes 196616 | tf_op jit(solution)/shard_map/ppermute | solution.py:32
  32.8 5.4 %collective-permute-start.13 = (bf16[2,1,128,128]{3,2,1,0:T(8,128)(2,1)S(1)}, bf16[2,1,128,128]{3,2,1,0:T(8,128)(2,1)S(1)}, u32[]{:S(2)}, u32[]{:S(2)}) collective-permute-start(bf16[2,1,128,128]{3,2,1,0:T(8,128)(2,1)S(1)} %get-tuple-element.64), channel_id=1, source_target_pairs={{0,12},{4,8},{8,4},{12,0},{16,28},{20,24},{24,20},{28,16},{1,13},{... | collective-permute-start | bytes 196616 | tf_op jit(solution)/shard_map/ppermute | solution.py:32
  34.2 5.0 %collective-permute-start.11 = (bf16[2,1,128,128]{3,2,1,0:T(8,128)(2,1)S(1)}, bf16[2,1,128,128]{3,2,1,0:T(8,128)(2,1)S(1)}, u32[]{:S(2)}, u32[]{:S(2)}) collective-permute-start(bf16[2,1,128,128]{3,2,1,0:T(8,128)(2,1)S(1)} %get-tuple-element.62.after_ref), channel_id=1, source_target_pairs={{0,4},{4,0},{8,12},{12,8},{16,20},{20,16},{24,28},{28,24},{1,5},{5... | collective-permute-start | bytes 196616 | tf_op jit(solution)/shard_map/ppermute | solution.py:32
  39.3 6.1 %collective-permute-start.17 = (bf16[1,128,128]{2,1,0:T(8,128)(2,1)S(1)}, bf16[1,128,128]{2,1,0:T(8,128)(2,1)S(1)}, u32[]{:S(2)}, u32[]{:S(2)}) collective-permute-start(bf16[1,128,128]{2,1,0:T(8,128)(2,1)S(1)} %get-tuple-element.75), channel_id=1, source_target_pairs={{0,16},{4,20},{8,24},{12,28},{16,0},{20,4},{24,8},{28,12},{1,17},{... | collective-permute-start | bytes 98312 | tf_op jit(solution)/shard_map/ppermute | solution.py:32
  41.9 7.1 %collective-permute-start.14 = (bf16[5,128,128]{2,1,0:T(8,128)(2,1)S(1)}, bf16[5,128,128]{2,1,0:T(8,128)(2,1)S(1)}, u32[]{:S(2)}, u32[]{:S(2)}) collective-permute-start(bf16[5,128,128]{2,1,0:T(8,128)(2,1)S(1)} %get-tuple-element.71.refs_0_), channel_id=1, source_target_pairs={{0,4},{4,0},{8,12},{12,8},{16,20},{20,16},{24,28},{28,24},{1,5},{5... | collective-permute-start | bytes 491528 | tf_op jit(solution)/shard_map/ppermute | solution.py:32
  42.7 5.0 %collective-permute-start.16 = (bf16[1,128,128]{2,1,0:T(8,128)(2,1)S(1)}, bf16[1,128,128]{2,1,0:T(8,128)(2,1)S(1)}, u32[]{:S(2)}, u32[]{:S(2)}) collective-permute-start(bf16[1,128,128]{2,1,0:T(8,128)(2,1)S(1)} %get-tuple-element.72), channel_id=1, source_target_pairs={{0,12},{4,8},{8,4},{12,0},{16,28},{20,24},{24,20},{28,16},{1,13},{... | collective-permute-start | bytes 98312 | tf_op jit(solution)/shard_map/ppermute | solution.py:32
  44.8 4.1 %collective-permute-start.15 = (bf16[1,128,128]{2,1,0:T(8,128)(2,1)S(1)}, bf16[1,128,128]{2,1,0:T(8,128)(2,1)S(1)}, u32[]{:S(2)}, u32[]{:S(2)}) collective-permute-start(bf16[1,128,128]{2,1,0:T(8,128)(2,1)S(1)} %get-tuple-element.72), channel_id=1, source_target_pairs={{0,8},{4,12},{8,0},{12,4},{16,24},{20,28},{24,16},{28,20},{1,9},{5... | collective-permute-start | bytes 98312 | tf_op jit(solution)/shard_map/ppermute | solution.py:32
  45.4 6.2 %collective-permute-start.20 = (bf16[1,128,128]{2,1,0:T(8,128)(2,1)S(1)}, bf16[1,128,128]{2,1,0:T(8,128)(2,1)S(1)}, u32[]{:S(2)}, u32[]{:S(2)}) collective-permute-start(bf16[1,128,128]{2,1,0:T(8,128)(2,1)S(1)} %shard_map.96.refs_0_), channel_id=1, source_target_pairs={{0,12},{4,8},{8,4},{12,0},{16,28},{20,24},{24,20},{28,16},{1,13},{... | collective-permute-start | bytes 98312 | tf_op jit(solution)/shard_map/ppermute | solution.py:32
  47.2 4.4 %collective-permute-start.19 = (bf16[1,128,128]{2,1,0:T(8,128)(2,1)S(1)}, bf16[1,128,128]{2,1,0:T(8,128)(2,1)S(1)}, u32[]{:S(2)}, u32[]{:S(2)}) collective-permute-start(bf16[1,128,128]{2,1,0:T(8,128)(2,1)S(1)} %shard_map.96.refs_0_), channel_id=1, source_target_pairs={{0,8},{4,12},{8,0},{12,4},{16,24},{20,28},{24,16},{28,20},{1,9},{5... | collective-permute-start | bytes 98312 | tf_op jit(solution)/shard_map/ppermute | solution.py:32
  47.6 4.0 %collective-permute-start.18 = (bf16[1,128,128]{2,1,0:T(8,128)(2,1)S(1)}, bf16[1,128,128]{2,1,0:T(8,128)(2,1)S(1)}, u32[]{:S(2)}, u32[]{:S(2)}) collective-permute-start(bf16[1,128,128]{2,1,0:T(8,128)(2,1)S(1)} %shard_map.96.refs_0_), channel_id=1, source_target_pairs={{0,4},{4,0},{8,12},{12,8},{16,20},{20,16},{24,28},{28,24},{1,5},{5... | collective-permute-start | bytes 98312 | tf_op jit(solution)/shard_map/ppermute | solution.py:32
